TPU v7x, 32 devices: a whole 2x2x4 slice. The times are simulated.
32 devices in a mesh: table: 8 (over z, core), seq: 4 (over y, x).
Axes of the slice: x: 2, y: 2, z: 4, core: 2. Of those that a mesh axis runs over, the one named last changes fastest.
Arguments:
- item_ids: int32 [32768], P('seq'), may hold values from 0 to 131071, as said below
- item_table: bfloat16 [131072, 512], P('seq', 'table'), may hold values from -6 to 6
- group_counts: int32 [8, 4, 8], replicated, may hold values from 0 to 192, as said below
- lengths: int32 [8], replicated, may hold values from 128 to 512
- history: bfloat16 [8, 2, 2, 512, 512], P('table', None, None, 'seq'), may hold values from -6 to 6
- w_in: bfloat16 [512, 2048], replicated, may hold values from -0.25 to 0.25
- w_out: bfloat16 [2048, 512], replicated, may hold values from -0.125 to 0.125
- w_proj: bfloat16 [2, 512, 1024], replicated, may hold values from -0.25 to 0.25
- w_back: bfloat16 [2, 512, 512], replicated, may hold values from -0.25 to 0.25
Outputs:
- ranked_states: bfloat16 [49152, 512], P(('table', 'seq'))
Inputs may be any that keep to these rules, and one draw needn't show every extreme that they name: `item_ids`: the ids of the 8192 candidates of index s of seq lie in s * 32768 to (s + 1) * 32768 - 1. Each group_counts[t, s, :] sums to 1024; every sender has some entry equal to 192; on some index s every t sends 192 to one group.
All inputs are finite; a program needn't handle non-finite values.
Results may differ from a plain program's by a relative error of at most 0.013.
Values may be sent and summed in bfloat16 or wider, within the bound.
No kernel may reach another device: no remote copies, remote signals or barrier semaphores. Data moves between devices by JAX's collectives and lax.ppermute only.
A program may use at most 128 MiB of HBM per device.

v0:
```python
import functools

import jax
import jax.numpy as jnp
from jax import lax
from jax.experimental import pallas as pl
from jax.experimental.pallas import tpu as pltpu
from jax.sharding import PartitionSpec as P

HEADS = 8
LANES = 128
UNROLL = 32
MIB = 1 << 20
ANY = pl.BlockSpec(memory_space=pl.ANY)
SMEM = pl.BlockSpec(memory_space=pltpu.SMEM)
VMEM = pl.BlockSpec(memory_space=pltpu.VMEM)


def lookup_kernel(
    geometry, ids, counts, table_t, out, table, rows_major, picked, id_vector, local_ids, held, sems
):
    low, high = geometry
    columns, vocab = table_t.shape
    groups = counts.shape[0]
    id_count = ids.shape[0]
    row_count = id_count // groups
    packing = LANES // columns
    shard = lax.axis_index("seq")
    get_ids = pltpu.make_async_copy(ids, id_vector, sems.at[0])
    get_ids.start()
    get_counts = pltpu.make_async_copy(counts, held, sems.at[1])
    get_counts.start()
    cuts = 8
    block = vocab // cuts
    get_table = [
        pltpu.make_async_copy(
            table_t.at[:, pl.ds(cut * block, block)],
            table.at[:, pl.ds(cut * block, block)],
            sems.at[3 + cut],
        )
        for cut in range(cuts)
    ]
    for copy in get_table:
        copy.start()
    get_ids.wait()
    id_vector[...] = id_vector[...] - shard * vocab
    put_ids = pltpu.make_async_copy(id_vector, local_ids.at[pl.ds(0, id_count)], sems.at[2])
    put_ids.start()
    for k in range(UNROLL):
        local_ids[id_count + k] = 0
    inner = 1024
    for cut in range(cuts):
        get_table[cut].wait()

        def turn(step, carry, cut=cut):
            at = pl.multiple_of(cut * block + step * inner, inner)
            piece = table[:, pl.ds(at, inner)]
            piece = jnp.concatenate([piece] * packing, axis=0)
            rows_major[pl.ds(at, inner), :] = piece.T.astype(jnp.float32)
            return carry

        lax.fori_loop(0, block // inner, turn, 0)
    get_counts.wait()
    put_ids.wait()

    def sender(sender_id, starts):
        source = sender_id * row_count
        new_starts = []
        for group in range(groups):
            amount = held[sender_id, shard, group]
            start = starts[group]
            first = jnp.maximum(start, low)
            wanted = jnp.minimum(start + amount, high) - first
            from_id = source + (first - start)
            target = first - low

            def several(size):
                def body(step, carry):
                    found = [
                        rows_major[pl.ds(local_ids[from_id + step * size + k], 1), :]
                        for k in range(size)
                    ]
                    for k in range(size):
                        picked[group, pl.ds(target + step * size + k, 1), :] = found[k]
                    return carry

                return body

            wanted = jnp.maximum(wanted, 0)
            rounds = wanted // UNROLL
            lax.fori_loop(0, rounds, several(UNROLL), 0)
            lax.fori_loop(rounds * (UNROLL // 8), (wanted + 7) // 8, several(8), 0)
            source = source + amount
            new_starts.append(start + amount)
        return tuple(new_starts)

    lax.fori_loop(0, groups, sender, (jnp.int32(0),) * groups)

    part = out.shape[1]
    lane = lax.broadcasted_iota(jnp.int32, (part, LANES), 1) // columns

    def pack(group, carry):
        value = picked[group, pl.ds(0, part), :]
        for piece in range(1, packing):
            value = jnp.where(lane == piece, picked[group, pl.ds(piece * part, part), :], value)
        out[group] = value.astype(jnp.bfloat16)
        return carry

    lax.fori_loop(0, groups, pack, 0)


def lookup(ids, counts, table_t, low, high):
    columns, vocab = table_t.shape
    packing = LANES // columns
    groups = counts.shape[0]
    return pl.pallas_call(
        functools.partial(lookup_kernel, (low, high)),
        out_shape=jax.ShapeDtypeStruct((groups, (high - low) // packing, LANES), jnp.bfloat16),
        in_specs=[ANY, ANY, ANY],
        out_specs=VMEM,
        scratch_shapes=[
            pltpu.VMEM((columns, vocab), jnp.bfloat16),
            pltpu.VMEM((vocab, LANES), jnp.float32),
            pltpu.VMEM((groups, high - low + UNROLL, LANES), jnp.float32),
            pltpu.VMEM(ids.shape, jnp.int32),
            pltpu.SMEM((ids.shape[0] + UNROLL,), jnp.int32),
            pltpu.SMEM(counts.shape, jnp.int32),
            pltpu.SemaphoreType.DMA((11,)),
        ],
        compiler_params=pltpu.CompilerParams(vmem_limit_bytes=62 * MIB),
        cost_estimate=pl.CostEstimate(
            flops=20_000_000_000, bytes_accessed=40_000_000, transcendentals=0
        ),
        name="lookup",
    )(ids, counts, table_t)


def cache_kernel(shards, lengths, *refs):
    pieces, (keys, values) = refs[: 2 * shards], refs[2 * shards :]
    layers, piece_rows, width = pieces[0].shape
    positions = shards * piece_rows
    pair = 2 * width // HEADS
    shard = lax.axis_index("seq")
    limit = lengths[lax.axis_index("table")]
    lane = lax.broadcasted_iota(jnp.int32, (positions, pair), 1)
    row = lax.broadcasted_iota(jnp.int32, (piece_rows, pair), 0)
    place = jnp.concatenate([row + (shard ^ k) * piece_rows for k in range(shards)], axis=0)
    kept = place < limit
    scale = 0.5 * (width // HEADS) ** -0.5
    for layer in range(layers):
        for block in range(HEADS // 2):
            columns = pl.ds(block * pair, pair)
            for kind in range(2):
                whole = jnp.concatenate(
                    [pieces[kind * shards + k][layer, :, columns] for k in range(shards)], axis=0
                ).astype(jnp.float32)
                for half in range(2):
                    mine = kept & ((lane // (pair // 2)) == half)
                    spot = pl.ds(half * positions, positions)
                    if kind == 0:
                        value = jnp.where(mine, whole * scale, 0.0).astype(jnp.bfloat16)
                        keys[layer, block, :, spot] = value.T
                    else:
                        value = jnp.where(mine, whole, 0.0).astype(jnp.bfloat16)
                        values[layer, block, spot, :] = value


def spread_cache(history, lengths):
    shards = lax.axis_size("seq")
    bits = [1 << k for k in range(shards.bit_length() - 1)]
    kinds = []
    for kind in range(2):
        held = {0: history[0, :, kind]}
        for bit in bits if kind == 0 else bits[::-1]:
            route = [(i, i ^ bit) for i in range(shards)]
            held.update({k ^ bit: lax.ppermute(v, "seq", route) for k, v in list(held.items())})
        kinds.append(held)
    pieces = [kinds[kind][index] for kind in range(2) for index in range(shards)]
    layers, piece_rows, width = pieces[0].shape
    pair, positions = 2 * width // HEADS, 2 * piece_rows * shards
    return pl.pallas_call(
        functools.partial(cache_kernel, shards),
        out_shape=(
            jax.ShapeDtypeStruct((layers, HEADS // 2, pair, positions), jnp.bfloat16),
            jax.ShapeDtypeStruct((layers, HEADS // 2, positions, pair), jnp.bfloat16),
        ),
        in_specs=[SMEM] + [VMEM] * len(pieces),
        out_specs=(VMEM, VMEM),
        compiler_params=pltpu.CompilerParams(vmem_limit_bytes=32 * MIB),
        name="cache",
    )(lengths, *pieces)


def half_silu(half):
    return half + half * jnp.tanh(half)


def dot(left, right):
    return jnp.dot(left, right, preferred_element_type=jnp.float32)


def row_mean(values):
    width = values.shape[1]
    partial = sum(values[:, at : at + LANES] for at in range(0, width, LANES))
    high = partial.astype(jnp.bfloat16)
    low = (partial - high.astype(jnp.float32)).astype(jnp.bfloat16)
    ones = jnp.full((2 * LANES, LANES), 1.0 / width, jnp.bfloat16)
    mean = dot(jnp.concatenate([high, low], axis=1), ones)
    return jnp.concatenate([mean] * (width // LANES), axis=1)


def normalized(values):
    centred = values - row_mean(values)
    return centred * lax.rsqrt(row_mean(centred * centred) + 1e-06)


def rank_kernel(low, capacity, done, counts, pieces, *refs):
    before, refs = refs[:done], refs[done:]
    sources, out, refs = refs[:6], refs[6], refs[7:]
    ranked, refs = (refs[0], refs[1:]) if done else (None, refs)
    held, sems = refs[:6], refs[6]
    keys, values, w_in, w_out, w_proj, w_back = held
    groups, part, _ = pieces.shape
    width = w_in.shape[0]
    packing = groups * LANES // width
    columns = LANES // packing
    tile = part * packing
    table_index = lax.axis_index("table")
    shard = lax.axis_index("seq")
    filled = lax.fori_loop(
        0, groups, lambda t, n: n + counts[t, shard, table_index], jnp.int32(0)
    )

    def keep(states):
        if done:
            for block in range(width // LANES):
                ranked[block, pl.ds(low, tile), :] = states[
                    :, block * LANES : (block + 1) * LANES
                ].astype(jnp.float32)
        else:
            out[...] = states

    if done:
        at = 0
        for piece in before:
            for block in range(width // LANES):
                ranked[block, pl.ds(at, piece.shape[0]), :] = piece[
                    :, pl.ds(block * LANES, LANES)
                ].astype(jnp.float32)
            at += piece.shape[0]

    @pl.when(low < filled)
    def _():
        copies = [
            pltpu.make_async_copy(sources[k], held[k], sems.at[k]) for k in (2, 3, 4, 0, 1, 5)
        ]
        for copy in copies:
            copy.start()
        lane = lax.broadcasted_iota(jnp.int32, (part, LANES), 1) // columns
        row = lax.broadcasted_iota(jnp.int32, (part, LANES), 0)
        rows = []
        for piece in range(packing):
            wanted = row + (low + piece * part) < filled
            blocks = []
            for block in range(width // LANES):
                value = None
                for spot in range(packing):
                    source = pieces[block * packing + spot].astype(jnp.float32)
                    turn = (spot - piece) % packing * columns
                    if turn:
                        source = pltpu.roll(source, turn, 1)
                    value = source if value is None else jnp.where(lane == spot, source, value)
                blocks.append(jnp.where(wanted, value, 0.0))
            rows.append(jnp.concatenate(blocks, axis=1))
        embedded = jnp.concatenate(rows, axis=0)
        embedded16 = embedded.astype(jnp.bfloat16)
        total = embedded
        chunk = width
        for copy in copies[:2]:
            copy.wait()
        for at in range(0, w_in.shape[1], chunk):
            half = dot(embedded16, w_in[:, at : at + chunk]) * 0.5
            hidden = half_silu(half).astype(jnp.bfloat16)
            total = total + dot(hidden, w_out[at : at + chunk, :])
        states = total.astype(jnp.bfloat16)
        pair = keys.shape[2]
        for copy in copies[2:]:
            copy.wait()
        for layer in range(w_proj.shape[0]):
            normed = normalized(states.astype(jnp.float32)).astype(jnp.bfloat16)
            gate = half_silu(dot(normed, w_proj[layer, :, :width]) * 0.5)
            queries = half_silu(dot(normed, w_proj[layer, :, width:]) * 0.5).astype(jnp.bfloat16)
            attended = []
            for block in range(HEADS // 2):
                query = queries[:, block * pair : (block + 1) * pair]
                weights = half_silu(dot(query, keys[layer, block])).astype(jnp.bfloat16)
                attended.append(dot(weights, values[layer, block]))
            attended = jnp.concatenate(attended, axis=1)
            mixed = (normalized(attended) * gate).astype(jnp.bfloat16)
            states = (states.astype(jnp.float32) + dot(mixed, w_back[layer])).astype(jnp.bfloat16)
        keep(states)

    if done:
        row = lax.broadcasted_iota(jnp.int32, (capacity, LANES), 0)

        def slot_block(sender, start):
            amount = counts[sender, shard, table_index]
            for block in range(width // LANES):
                value = ranked[block, pl.ds(start, capacity), :]
                out[
                    pl.ds(pl.multiple_of(sender * capacity, capacity), capacity),
                    block * LANES : (block + 1) * LANES,
                ] = jnp.where(row < amount, value, 0.0).astype(jnp.bfloat16)
            return start + amount

        lax.fori_loop(0, groups, slot_block, jnp.int32(0))


def rank(counts, pieces, before, sources, low, capacity):
    groups, part, _ = pieces.shape
    width = sources[2].shape[0]
    tile = part * groups * LANES // width
    total = groups * capacity
    done = len(before)
    scratch = [pltpu.VMEM(source.shape, source.dtype) for source in sources]
    if done:
        scratch = [pltpu.VMEM((width // LANES, total + capacity, LANES), jnp.float32)] + scratch
    return pl.pallas_call(
        functools.partial(rank_kernel, low, capacity, done),
        out_shape=jax.ShapeDtypeStruct((total if done else tile, width), jnp.bfloat16),
        in_specs=[SMEM, VMEM] + [VMEM] * done + [ANY] * len(sources),
        out_specs=VMEM,
        scratch_shapes=scratch + [pltpu.SemaphoreType.DMA((len(sources),))],
        compiler_params=pltpu.CompilerParams(vmem_limit_bytes=62 * MIB),
        cost_estimate=pl.CostEstimate(
            flops=20_000_000_000, bytes_accessed=20_000_000, transcendentals=0
        ),
        name="rank",
    )(counts, pieces, *before, *sources)


def local(item_ids, item_table, group_counts, lengths, history, w_in, w_out, w_proj, w_back):
    groups = lax.axis_size("table")
    row_count = item_ids.shape[0] // groups
    capacity = 3 * row_count // (2 * groups)
    total = groups * capacity
    cuts = (0, total * 7 // 12, total)
    table_t = item_table.T
    pieces = []
    for low, high in zip(cuts, cuts[1:]):
        found = lookup(item_ids, group_counts, table_t, low, high)
        pieces.append(lax.all_to_all(found, "table", split_axis=0, concat_axis=0, tiled=True))
    keys, values = spread_cache(history, lengths)
    sources = (keys, values, w_in, w_out, w_proj, w_back)
    states = []
    for part, low in enumerate(cuts[:-1]):
        before = states if part == len(cuts) - 2 else []
        states = states + [rank(group_counts, pieces[part], before, sources, low, capacity)]
    return states[-1]


def solution(mesh):
    placed = (
        P("seq"),
        P("seq", "table"),
        P(),
        P(),
        P("table", None, None, "seq", None),
        P(),
        P(),
        P(),
        P(),
    )
    return jax.shard_map(
        local, mesh=mesh, in_specs=placed, out_specs=P(("table", "seq"), None), check_vma=False
    )
```

profile of v0, /device:TPU:1, one launch (start us, length us, event | category | flops | bytes accessed | tf_op | source)
XLA Modules:
  0.0 96.8 jit_solution(3045865290706336404)
XLA Ops:
  0.0 1.1 %slice_bitcast_fusion = (bf16[2,128,512]{2,1,0:T(8,128)(2,1)S(1)}, bf16[2,128,512]{2,1,0:T(8,128)(2,1)S(1)}) fusion(bf16[1,2,2,128,512]{4,3,2,1,0:T(8,128)(2,1)} %param.13), kind=kLoop, calls=%fused_computation | loop fusion | bytes 1048576 | tf_op jit(solution)/shard_map/squeeze | solution.py:173
  1.1 2.1 %collective-permute-start = (bf16[2,128,512]{2,1,0:T(8,128)(2,1)S(1)}, bf16[2,128,512]{2,1,0:T(8,128)(2,1)S(1)}, u32[]{:S(2)}, u32[]{:S(2)}) collective-permute-start(bf16[2,128,512]{2,1,0:T(8,128)(2,1)S(1)} %get-tuple-element.10.refs_0_), channel_id=1, source_target_pairs={{0,1},{1,0},{2,3},{3,2},{4,5},{5,4},{6,7},{7,6},{8,9},{9,8},{10,11... | collective-permute-start | bytes 786440 | tf_op jit(solution)/shard_map/ppermute | solution.py:176
  3.2 1.2 %collective-permute-start.1 = (bf16[2,128,512]{2,1,0:T(8,128)(2,1)S(1)}, bf16[2,128,512]{2,1,0:T(8,128)(2,1)S(1)}, u32[]{:S(2)}, u32[]{:S(2)}) collective-permute-start(bf16[2,128,512]{2,1,0:T(8,128)(2,1)S(1)} %get-tuple-element.10.refs_0_), channel_id=1, source_target_pairs={{0,2},{1,3},{2,0},{3,1},{4,6},{5,7},{6,4},{7,5},{8,10},{9,11},{10,... | collective-permute-start | bytes 786440 | tf_op jit(solution)/shard_map/ppermute | solution.py:176
  4.4 0.2 collective-permute-start.4
  4.6 0.1 collective-permute-start.3
  4.7 15.3 %lookup.3 = bf16[8,448,128]{2,1,0:T(8,128)(2,1)} custom-call(s32[8192]{0:T(1024)} %ids.3, s32[8,4,8]{2,1,0:T(4,128)} %counts.7, bf16[64,32768]{1,0:T(8,128)(2,1)} %bitcast.9), custom_call_target="tpu_custom_call" | custom-call | flops 20000000000 | bytes 40000000 | tf_op jit(solution)/shard_map/lookup/pallas_call | solution.py:116
  20.1 6.9 %all-to-all-start.1 = ((bf16[8,448,128]{2,1,0:T(8,128)(2,1)}), bf16[8,448,128]{2,1,0:T(8,128)(2,1)}, u32[]{:S(2)}, u32[]{:S(2)}) async-start(bf16[8,448,128]{2,1,0:T(8,128)(2,1)} %lookup.3), calls=%async_computation.1 | async-start | bytes 1835008 | tf_op jit(solution)/shard_map/all_to_all | solution.py:352
  26.9 0.0 copy-start
  26.9 0.0 collective-permute-done.refs_1_
  26.9 1.3 %collective-permute-start.2 = (bf16[2,128,512]{2,1,0:T(8,128)(2,1)S(1)}, bf16[2,128,512]{2,1,0:T(8,128)(2,1)S(1)}, u32[]{:S(2)}, u32[]{:S(2)}) collective-permute-start(bf16[2,128,512]{2,1,0:T(8,128)(2,1)S(1)} %collective-permute-done.refs_1_), channel_id=1, source_target_pairs={{0,2},{1,3},{2,0},{3,1},{4,6},{5,7},{6,4},{7,5},{8,10},{9,11},{10,... | collective-permute-start | bytes 786440 | tf_op jit(solution)/shard_map/ppermute | solution.py:176
  28.2 0.0 collective-permute-done.4.refs_6_
  28.2 1.2 %collective-permute-start.5 = (bf16[2,128,512]{2,1,0:T(8,128)(2,1)S(1)}, bf16[2,128,512]{2,1,0:T(8,128)(2,1)}, u32[]{:S(2)}, u32[]{:S(2)}) collective-permute-start(bf16[2,128,512]{2,1,0:T(8,128)(2,1)S(1)} %collective-permute-done.4.refs_6_), channel_id=1, source_target_pairs={{0,1},{1,0},{2,3},{3,2},{4,5},{5,4},{6,7},{7,6},{8,9},{9,8},{10,11... | collective-permute-start | bytes 786440 | tf_op jit(solution)/shard_map/ppermute | solution.py:176
  29.4 9.1 %lookup.2 = bf16[8,320,128]{2,1,0:T(8,128)(2,1)} custom-call(s32[8192]{0:T(1024)} %ids.3, s32[8,4,8]{2,1,0:T(4,128)} %counts.7, bf16[64,32768]{1,0:T(8,128)(2,1)} %bitcast.10), custom_call_target="tpu_custom_call" | custom-call | flops 20000000000 | bytes 40000000 | tf_op jit(solution)/shard_map/lookup/pallas_call | solution.py:116
  38.5 0.0 collective-permute-done.1.refs_2_
  38.5 0.0 collective-permute-done.3.refs_5_
  38.5 0.0 collective-permute-done.2.refs_3_
  38.5 0.0 collective-permute-done.5.refs_7_
  38.5 0.0 copy-done
  38.5 2.0 %cache.1 = (bf16[2,4,128,1024]{3,2,1,0:T(8,128)(2,1)S(1)}, bf16[2,4,1024,128]{3,2,1,0:T(8,128)(2,1)S(1)}) custom-call(s32[8]{0:T(128)S(1)} %copy-done, bf16[2,128,512]{2,1,0:T(8,128)(2,1)S(1)} %get-tuple-element.10.refs_0_, bf16[2,128,512]{2,1,0:T(8,128)(2,1)S(1)} %collective-permute-done.refs_1_, bf16[2,128,512]{2,1,0:T(8,128)(2,1)S(1)} %collective-permute-done.1.refs_2_, ...), custom_call_target="tpu_custom_call" | custom-call | tf_op jit(solution)/shard_map/cache/pallas_call | solution.py:181
  40.5 0.0 copy-start.1
  40.5 1.3 %copy-done.1 = bf16[2,4,128,1024]{3,2,1,0:T(8,128)(2,1)} copy-done((bf16[2,4,128,1024]{3,2,1,0:T(8,128)(2,1)}, bf16[2,4,128,1024]{3,2,1,0:T(8,128)(2,1)S(1)}, u32[]{:S(2)}) %copy-start.1) | copy-done | bytes 2097176
  41.9 0.0 copy-start.2
  41.9 1.3 %copy-done.2 = bf16[2,4,1024,128]{3,2,1,0:T(8,128)(2,1)} copy-done((bf16[2,4,1024,128]{3,2,1,0:T(8,128)(2,1)}, bf16[2,4,1024,128]{3,2,1,0:T(8,128)(2,1)S(1)}, u32[]{:S(2)}) %copy-start.2) | copy-done | bytes 2097176
  43.2 6.8 %all-to-all-done.1.pieces = bf16[8,448,128]{2,1,0:T(8,128)(2,1)} async-done(((bf16[8,448,128]{2,1,0:T(8,128)(2,1)}), bf16[8,448,128]{2,1,0:T(8,128)(2,1)}, u32[]{:S(2)}, u32[]{:S(2)}) %all-to-all-start.1) | async-done | bytes 917536 | tf_op jit(solution)/shard_map/all_to_all | solution.py:352
  49.9 4.3 %all-to-all-start = ((bf16[8,320,128]{2,1,0:T(8,128)(2,1)}), bf16[8,320,128]{2,1,0:T(8,128)(2,1)S(1)}, u32[]{:S(2)}, u32[]{:S(2)}) async-start(bf16[8,320,128]{2,1,0:T(8,128)(2,1)} %lookup.2), calls=%async_computation | async-start | bytes 1310720 | tf_op jit(solution)/shard_map/all_to_all | solution.py:352
  54.3 23.1 %rank.2.refs_0_ = bf16[896,512]{1,0:T(8,128)(2,1)} custom-call(s32[8,4,8]{2,1,0:T(4,128)} %counts.7, bf16[8,448,128]{2,1,0:T(8,128)(2,1)} %all-to-all-done.1.pieces, bf16[2,4,128,1024]{3,2,1,0:T(8,128)(2,1)} %copy-done.1, bf16[2,4,1024,128]{3,2,1,0:T(8,128)(2,1)} %copy-done.2, bf16[512,2048]{1,0:T(8,128)(2,1)} %refs_3_.3, bf16[2048,512]{1,0:T(8,128)(2,1)} %refs_4_.3, ...), custom_call_target="tpu_custom_call" | custom-call | flops 20000000000 | bytes 20000000 | tf_op jit(solution)/shard_map/rank/pallas_call | solution.py:328
  77.3 0.0 all-to-all-done.pieces
  77.4 0.0 copy-start.3
  77.4 0.8 copy-done.3
  78.2 18.4 %rank.3 = bf16[1536,512]{1,0:T(8,128)(2,1)} custom-call(s32[8,4,8]{2,1,0:T(4,128)} %counts.7, bf16[8,320,128]{2,1,0:T(8,128)(2,1)} %copy-done.3, bf16[896,512]{1,0:T(8,128)(2,1)} %rank.2.refs_0_, bf16[2,4,128,1024]{3,2,1,0:T(8,128)(2,1)} %copy-done.1, bf16[2,4,1024,128]{3,2,1,0:T(8,128)(2,1)} %copy-done.2, bf16[512,2048]{1,0:T(8,128)(2,1)} %refs_3_.3, ...), custom_call_target="tpu_custom_call" | custom-call | flops 20000000000 | bytes 20000000 | tf_op jit(solution)/shard_map/rank/pallas_call | solution.py:328
Async XLA Ops:
  1.1 25.9 %collective-permute-start = (bf16[2,128,512]{2,1,0:T(8,128)(2,1)S(1)}, bf16[2,128,512]{2,1,0:T(8,128)(2,1)S(1)}, u32[]{:S(2)}, u32[]{:S(2)}) collective-permute-start(bf16[2,128,512]{2,1,0:T(8,128)(2,1)S(1)} %get-tuple-element.10.refs_0_), channel_id=1, source_target_pairs={{0,1},{1,0},{2,3},{3,2},{4,5},{5,4},{6,7},{7,6},{8,9},{9,8},{10,11... | collective-permute-start | bytes 786440 | tf_op jit(solution)/shard_map/ppermute | solution.py:176
  3.2 35.3 %collective-permute-start.1 = (bf16[2,128,512]{2,1,0:T(8,128)(2,1)S(1)}, bf16[2,128,512]{2,1,0:T(8,128)(2,1)S(1)}, u32[]{:S(2)}, u32[]{:S(2)}) collective-permute-start(bf16[2,128,512]{2,1,0:T(8,128)(2,1)S(1)} %get-tuple-element.10.refs_0_), channel_id=1, source_target_pairs={{0,2},{1,3},{2,0},{3,1},{4,6},{5,7},{6,4},{7,5},{8,10},{9,11},{10,... | collective-permute-start | bytes 786440 | tf_op jit(solution)/shard_map/ppermute | solution.py:176
  4.4 23.8 %collective-permute-start.4 = (bf16[2,128,512]{2,1,0:T(8,128)(2,1)S(1)}, bf16[2,128,512]{2,1,0:T(8,128)(2,1)S(1)}, u32[]{:S(2)}, u32[]{:S(2)}) collective-permute-start(bf16[2,128,512]{2,1,0:T(8,128)(2,1)S(1)} %get-tuple-element.9.refs_4_), channel_id=1, source_target_pairs={{0,2},{1,3},{2,0},{3,1},{4,6},{5,7},{6,4},{7,5},{8,10},{9,11},{10,... | collective-permute-start | bytes 786440 | tf_op jit(solution)/shard_map/ppermute | solution.py:176
  4.6 33.8 %collective-permute-start.3 = (bf16[2,128,512]{2,1,0:T(8,128)(2,1)S(1)}, bf16[2,128,512]{2,1,0:T(8,128)(2,1)S(1)}, u32[]{:S(2)}, u32[]{:S(2)}) collective-permute-start(bf16[2,128,512]{2,1,0:T(8,128)(2,1)S(1)} %get-tuple-element.9.refs_4_), channel_id=1, source_target_pairs={{0,1},{1,0},{2,3},{3,2},{4,5},{5,4},{6,7},{7,6},{8,9},{9,8},{10,11... | collective-permute-start | bytes 786440 | tf_op jit(solution)/shard_map/ppermute | solution.py:176
  20.1 29.9 %all-to-all-start.1 = ((bf16[8,448,128]{2,1,0:T(8,128)(2,1)}), bf16[8,448,128]{2,1,0:T(8,128)(2,1)}, u32[]{:S(2)}, u32[]{:S(2)}) async-start(bf16[8,448,128]{2,1,0:T(8,128)(2,1)} %lookup.3), calls=%async_computation.1 | async-start | bytes 1835008 | tf_op jit(solution)/shard_map/all_to_all | solution.py:352
  26.9 11.6 %copy-start = (s32[8]{0:T(128)S(1)}, s32[8]{0:T(128)}, u32[]{:S(2)}) copy-start(s32[8]{0:T(128)} %lengths.1) | copy-start | bytes 100
  26.9 11.5 %collective-permute-start.2 = (bf16[2,128,512]{2,1,0:T(8,128)(2,1)S(1)}, bf16[2,128,512]{2,1,0:T(8,128)(2,1)S(1)}, u32[]{:S(2)}, u32[]{:S(2)}) collective-permute-start(bf16[2,128,512]{2,1,0:T(8,128)(2,1)S(1)} %collective-permute-done.refs_1_), channel_id=1, source_target_pairs={{0,2},{1,3},{2,0},{3,1},{4,6},{5,7},{6,4},{7,5},{8,10},{9,11},{10,... | collective-permute-start | bytes 786440 | tf_op jit(solution)/shard_map/ppermute | solution.py:176
  28.2 10.3 %collective-permute-start.5 = (bf16[2,128,512]{2,1,0:T(8,128)(2,1)S(1)}, bf16[2,128,512]{2,1,0:T(8,128)(2,1)}, u32[]{:S(2)}, u32[]{:S(2)}) collective-permute-start(bf16[2,128,512]{2,1,0:T(8,128)(2,1)S(1)} %collective-permute-done.4.refs_6_), channel_id=1, source_target_pairs={{0,1},{1,0},{2,3},{3,2},{4,5},{5,4},{6,7},{7,6},{8,9},{9,8},{10,11... | collective-permute-start | bytes 786440 | tf_op jit(solution)/shard_map/ppermute | solution.py:176
  40.5 1.3 %copy-start.1 = (bf16[2,4,128,1024]{3,2,1,0:T(8,128)(2,1)}, bf16[2,4,128,1024]{3,2,1,0:T(8,128)(2,1)S(1)}, u32[]{:S(2)}) copy-start(bf16[2,4,128,1024]{3,2,1,0:T(8,128)(2,1)S(1)} %get-tuple-element.7.refs_0_.refs_1_) | copy-start | bytes 6291460
  41.9 1.3 %copy-start.2 = (bf16[2,4,1024,128]{3,2,1,0:T(8,128)(2,1)}, bf16[2,4,1024,128]{3,2,1,0:T(8,128)(2,1)S(1)}, u32[]{:S(2)}) copy-start(bf16[2,4,1024,128]{3,2,1,0:T(8,128)(2,1)S(1)} %get-tuple-element.8.refs_1_.refs_2_) | copy-start | bytes 6291460
  49.9 27.4 %all-to-all-start = ((bf16[8,320,128]{2,1,0:T(8,128)(2,1)}), bf16[8,320,128]{2,1,0:T(8,128)(2,1)S(1)}, u32[]{:S(2)}, u32[]{:S(2)}) async-start(bf16[8,320,128]{2,1,0:T(8,128)(2,1)} %lookup.2), calls=%async_computation | async-start | bytes 1310720 | tf_op jit(solution)/shard_map/all_to_all | solution.py:352
  77.4 0.8 copy-start.3
where the time goes:
time: 97.2 us; the launch traced here: 96.8 us
  Pallas kernels  67.9 us (70%)
  starting transfers between devices  17.2 us (18%)
  waiting for transfers between devices  6.78 us (7%)
  local copies, waits for them, and re-layouts  4.55 us (5%)
    pallas_call x2, Pallas kernels, rank(): pl.pallas_call(functools.partial(rank_kernel, low, capacity, done), out_s...  41.4 us
    pallas_call x2, Pallas kernels, lookup(): pl.pallas_call(functools.partial(lookup_kernel, (low, high)), out_shape=j...  24.4 us
    all_to_all x2, starting transfers between devices, local(): lax.all_to_all(found, 'table', split_axis=0, concat_axis=0, tiled=True)  11.2 us
    all_to_all x2, waiting for transfers between devices, local(): lax.all_to_all(found, 'table', split_axis=0, concat_axis=0, tiled=True)  6.76 us
    ppermute x6, starting transfers between devices, spread_cache(): lax.ppermute(v, 'seq', route)  6.07 us
    unnamed x8, local copies, waits for them, and re-layouts  3.49 us
    pallas_call x1, Pallas kernels, spread_cache(): pl.pallas_call(functools.partial(cache_kernel, shards), out_shape=(jax.Sh...  2.03 us
  transfers between devices with their start and end apart: 8, of which 1 were waited for; matrix products, arithmetic and copies ran while one was open for 0% of the time, Pallas kernels for 51%

commit v1 on v0

v1 whole, which is shorter than its diff:
```python
import functools

import jax
import jax.numpy as jnp
from jax import lax
from jax.experimental import pallas as pl
from jax.experimental.pallas import tpu as pltpu
from jax.sharding import PartitionSpec as P

HEADS = 8
LANES = 128
UNROLL = 64
MIB = 1 << 20
ANY = pl.BlockSpec(memory_space=pl.ANY)
SMEM = pl.BlockSpec(memory_space=pltpu.SMEM)
VMEM = pl.BlockSpec(memory_space=pltpu.VMEM)


def lookup_kernel(cuts, ids, counts, table_t, *refs):
    outs, refs = refs[: len(cuts) - 1], refs[len(cuts) - 1 :]
    table, rows_major, found, picked, id_vector, local_ids, held, sems = refs
    columns, vocab = table_t.shape
    groups = counts.shape[0]
    id_count = ids.shape[0]
    row_count = id_count // groups
    packing = LANES // columns
    capacity = cuts[-1] // groups
    shard = lax.axis_index("seq")
    get_ids = pltpu.make_async_copy(ids, id_vector, sems.at[0])
    get_ids.start()
    get_counts = pltpu.make_async_copy(counts, held, sems.at[1])
    get_counts.start()
    parts = 8
    block = vocab // parts
    get_table = [
        pltpu.make_async_copy(
            table_t.at[:, pl.ds(part * block, block)],
            table.at[:, pl.ds(part * block, block)],
            sems.at[3 + part],
        )
        for part in range(parts)
    ]
    for copy in get_table:
        copy.start()
    get_ids.wait()
    id_vector[...] = id_vector[...] - shard * vocab
    put_ids = pltpu.make_async_copy(id_vector, local_ids, sems.at[2])
    put_ids.start()
    inner = 1024
    for part in range(parts):
        get_table[part].wait()

        def turn(step, carry, part=part):
            at = pl.multiple_of(part * block + step * inner, inner)
            piece = table[:, pl.ds(at, inner)]
            piece = jnp.concatenate([piece] * packing, axis=0)
            rows_major[pl.ds(at, inner), :] = piece.T.astype(jnp.float32)
            return carry

        lax.fori_loop(0, block // inner, turn, 0)
    get_counts.wait()
    put_ids.wait()

    def gather(step, carry):
        at = pl.multiple_of(step * UNROLL, UNROLL)
        rows = [rows_major[pl.ds(local_ids[at + k], 1), :] for k in range(UNROLL)]
        for k in range(UNROLL):
            found[pl.ds(at + k, 1), :] = rows[k]
        return carry

    lax.fori_loop(0, id_count // UNROLL, gather, 0)

    def sender(sender_id, starts):
        source = sender_id * row_count
        new_starts = []
        for group in range(groups):
            amount = held[sender_id, shard, group]
            picked[group, pl.ds(starts[group], capacity), :] = found[pl.ds(source, capacity), :]
            source = source + amount
            new_starts.append(starts[group] + amount)
        return tuple(new_starts)

    lax.fori_loop(0, groups, sender, (jnp.int32(0),) * groups)

    def pack(group, carry):
        for low, out in zip(cuts, outs):
            part = out.shape[1]
            lane = lax.broadcasted_iota(jnp.int32, (part, LANES), 1) // columns
            value = picked[group, pl.ds(low, part), :]
            for piece in range(1, packing):
                more = picked[group, pl.ds(low + piece * part, part), :]
                value = jnp.where(lane == piece, more, value)
            out[group] = value.astype(jnp.bfloat16)
        return carry

    lax.fori_loop(0, groups, pack, 0)


def lookup(ids, counts, table_t, cuts):
    columns, vocab = table_t.shape
    packing = LANES // columns
    groups = counts.shape[0]
    total = cuts[-1]
    return pl.pallas_call(
        functools.partial(lookup_kernel, cuts),
        out_shape=tuple(
            jax.ShapeDtypeStruct((groups, (high - low) // packing, LANES), jnp.bfloat16)
            for low, high in zip(cuts, cuts[1:])
        ),
        in_specs=[ANY, ANY, ANY],
        out_specs=(VMEM,) * (len(cuts) - 1),
        scratch_shapes=[
            pltpu.VMEM((columns, vocab), jnp.bfloat16),
            pltpu.VMEM((vocab, LANES), jnp.float32),
            pltpu.VMEM((ids.shape[0] + total // groups, LANES), jnp.float32),
            pltpu.VMEM((groups, total + total // groups, LANES), jnp.float32),
            pltpu.VMEM(ids.shape, jnp.int32),
            pltpu.SMEM(ids.shape, jnp.int32),
            pltpu.SMEM(counts.shape, jnp.int32),
            pltpu.SemaphoreType.DMA((11,)),
        ],
        compiler_params=pltpu.CompilerParams(vmem_limit_bytes=62 * MIB),
        name="lookup",
    )(ids, counts, table_t)


def gather_history(history):
    shards = lax.axis_size("seq")
    bits = [1 << k for k in range(shards.bit_length() - 1)]
    pieces = []
    for kind in range(2):
        held = {0: history[0, :, kind]}
        for bit in bits if kind == 0 else bits[::-1]:
            route = [(i, i ^ bit) for i in range(shards)]
            held.update({k ^ bit: lax.ppermute(v, "seq", route) for k, v in list(held.items())})
        pieces += [held[index] for index in range(shards)]
    return pieces


def half_silu(half):
    return half + half * jnp.tanh(half)


def dot(left, right):
    return jnp.dot(left, right, preferred_element_type=jnp.float32)


def dot_rows(left, right):
    return lax.dot_general(
        left, right, (((1,), (1,)), ((), ())), preferred_element_type=jnp.float32
    )


def row_mean(values):
    width = values.shape[1]
    partial = sum(values[:, at : at + LANES] for at in range(0, width, LANES))
    high = partial.astype(jnp.bfloat16)
    low = (partial - high.astype(jnp.float32)).astype(jnp.bfloat16)
    ones = jnp.full((2 * LANES, LANES), 1.0 / width, jnp.bfloat16)
    mean = dot(jnp.concatenate([high, low], axis=1), ones)
    return jnp.concatenate([mean] * (width // LANES), axis=1)


def normalized(values):
    centred = values - row_mean(values)
    return centred * lax.rsqrt(row_mean(centred * centred) + 1e-06)


def rank_kernel(low, capacity, done, shards, counts, lengths, pieces, *refs):
    before, refs = refs[:done], refs[done:]
    history, refs = refs[: 2 * shards], refs[2 * shards :]
    weights, out, refs = refs[:4], refs[4], refs[5:]
    ranked, refs = (refs[0], refs[1:]) if done else (None, refs)
    keys, values, w_in, w_out, w_proj, w_back, sems = refs
    groups, part, _ = pieces.shape
    width = w_in.shape[0]
    packing = groups * LANES // width
    columns = LANES // packing
    tile = part * packing
    table_index = lax.axis_index("table")
    shard = lax.axis_index("seq")
    filled = lax.fori_loop(
        0, groups, lambda t, n: n + counts[t, shard, table_index], jnp.int32(0)
    )

    def keep(states):
        if done:
            for block in range(width // LANES):
                ranked[block, pl.ds(low, tile), :] = states[
                    :, block * LANES : (block + 1) * LANES
                ].astype(jnp.float32)
        else:
            out[...] = states

    if done:
        at = 0
        for piece in before:
            for block in range(width // LANES):
                ranked[block, pl.ds(at, piece.shape[0]), :] = piece[
                    :, pl.ds(block * LANES, LANES)
                ].astype(jnp.float32)
            at += piece.shape[0]

    @pl.when(low < filled)
    def _():
        chunk = width
        head, tail = pl.ds(0, chunk), pl.ds(chunk, w_in.shape[1] - chunk)
        views = [
            (weights[0].at[:, head], w_in.at[:, head]),
            (weights[1].at[head], w_out.at[head]),
            (weights[0].at[:, tail], w_in.at[:, tail]),
            (weights[1].at[tail], w_out.at[tail]),
            (weights[2], w_proj),
            (weights[3], w_back),
        ]
        piece_rows = keys.shape[1] // shards
        for k in range(2 * shards):
            place = pl.multiple_of((shard ^ (k % shards)) * piece_rows, piece_rows)
            target = (keys, values)[k // shards]
            views.append((history[k], target.at[:, pl.ds(place, piece_rows), :]))
        copies = [
            pltpu.make_async_copy(source, target, sems.at[k])
            for k, (source, target) in enumerate(views)
        ]
        for copy in copies[:4]:
            copy.start()
        lane = lax.broadcasted_iota(jnp.int32, (part, LANES), 1) // columns
        row = lax.broadcasted_iota(jnp.int32, (part, LANES), 0)
        rows = []
        for piece in range(packing):
            wanted = row + (low + piece * part) < filled
            blocks = []
            for block in range(width // LANES):
                value = None
                for spot in range(packing):
                    source = pieces[block * packing + spot].astype(jnp.float32)
                    turn = (spot - piece) % packing * columns
                    if turn:
                        source = pltpu.roll(source, turn, 1)
                    value = source if value is None else jnp.where(lane == spot, source, value)
                blocks.append(jnp.where(wanted, value, 0.0))
            rows.append(jnp.concatenate(blocks, axis=1))
        embedded = jnp.concatenate(rows, axis=0)
        embedded16 = embedded.astype(jnp.bfloat16)
        total = embedded
        for copy in copies[:2]:
            copy.wait()
        for copy in copies[4:]:
            copy.start()
        for at in range(0, w_in.shape[1], chunk):
            if at == chunk:
                for copy in copies[2:4]:
                    copy.wait()
            half = dot(embedded16, w_in[:, at : at + chunk]) * 0.5
            hidden = half_silu(half).astype(jnp.bfloat16)
            total = total + dot(hidden, w_out[at : at + chunk, :])
        states = total.astype(jnp.bfloat16)
        for copy in copies[4:]:
            copy.wait()
        pair = 2 * width // HEADS
        limit = lengths[table_index]
        cached = lax.broadcasted_iota(jnp.int32, keys.shape[1:], 0) < limit
        first = lax.broadcasted_iota(jnp.int32, (tile, pair), 1) < pair // 2
        scale = 0.5 * (width // HEADS) ** -0.5
        for layer in range(w_proj.shape[0]):
            normed = normalized(states.astype(jnp.float32)).astype(jnp.bfloat16)
            queries = half_silu(dot(normed, w_proj[layer, :, width:]) * 0.5) * scale
            queries = queries.astype(jnp.bfloat16)
            kept = jnp.where(cached, keys[layer], jnp.zeros((), jnp.bfloat16))

            def score(block):
                query = queries[:, block * pair : (block + 1) * pair]
                none = jnp.zeros((), jnp.bfloat16)
                both = jnp.concatenate(
                    [jnp.where(first, query, none), jnp.where(first, none, query)], axis=0
                )
                return dot_rows(both, kept[:, block * pair : (block + 1) * pair])

            attended = []
            scores = score(0)
            for block in range(HEADS // 2):
                following = score(block + 1) if block + 1 < HEADS // 2 else None
                weighted = half_silu(scores).astype(jnp.bfloat16)
                both = dot(weighted, values[layer, :, block * pair : (block + 1) * pair])
                attended.append(jnp.where(first, both[:tile], both[tile:]))
                scores = following
            attended = jnp.concatenate(attended, axis=1)
            gate = half_silu(dot(normed, w_proj[layer, :, :width]) * 0.5)
            mixed = (normalized(attended) * gate).astype(jnp.bfloat16)
            states = (states.astype(jnp.float32) + dot(mixed, w_back[layer])).astype(jnp.bfloat16)
        keep(states)

    if done:
        row = lax.broadcasted_iota(jnp.int32, (capacity, LANES), 0)

        def slot_block(sender, start):
            amount = counts[sender, shard, table_index]
            for block in range(width // LANES):
                value = ranked[block, pl.ds(start, capacity), :]
                out[
                    pl.ds(pl.multiple_of(sender * capacity, capacity), capacity),
                    block * LANES : (block + 1) * LANES,
                ] = jnp.where(row < amount, value, 0.0).astype(jnp.bfloat16)
            return start + amount

        lax.fori_loop(0, groups, slot_block, jnp.int32(0))


def rank(counts, lengths, pieces, before, history, weights, low, capacity):
    groups, part, _ = pieces.shape
    width = weights[0].shape[0]
    tile = part * groups * LANES // width
    total = groups * capacity
    done = len(before)
    layers, piece_rows, _ = history[0].shape
    shards = len(history) // 2
    scratch = [pltpu.VMEM((layers, shards * piece_rows, width), jnp.bfloat16)] * 2
    scratch += [pltpu.VMEM(weight.shape, weight.dtype) for weight in weights]
    scratch += [pltpu.SemaphoreType.DMA((len(weights) + 2 + len(history),))]
    if done:
        scratch = [pltpu.VMEM((width // LANES, total + capacity, LANES), jnp.float32)] + scratch
    return pl.pallas_call(
        functools.partial(rank_kernel, low, capacity, done, shards),
        out_shape=jax.ShapeDtypeStruct((total if done else tile, width), jnp.bfloat16),
        in_specs=[SMEM, SMEM, VMEM] + [VMEM] * done + [ANY] * (len(history) + len(weights)),
        out_specs=VMEM,
        scratch_shapes=scratch,
        compiler_params=pltpu.CompilerParams(vmem_limit_bytes=62 * MIB),
        cost_estimate=pl.CostEstimate(
            flops=20_000_000_000, bytes_accessed=20_000_000, transcendentals=0
        ),
        name="rank",
    )(counts, lengths, pieces, *before, *history, *weights)


def local(item_ids, item_table, group_counts, lengths, history, w_in, w_out, w_proj, w_back):
    groups = lax.axis_size("table")
    row_count = item_ids.shape[0] // groups
    capacity = 3 * row_count // (2 * groups)
    total = groups * capacity
    cuts = (0, total * 13 // 24, total)
    table_t = item_table.T
    found = lookup(item_ids, group_counts, table_t, cuts)
    pieces = [
        lax.all_to_all(chunk, "table", split_axis=0, concat_axis=0, tiled=True) for chunk in found
    ]
    history = gather_history(history)
    weights = (w_in, w_out, w_proj, w_back)
    states = []
    for low, chunk in zip(cuts, pieces):
        before = states if low == cuts[-2] else []
        states = states + [
            rank(group_counts, lengths, chunk, before, history, weights, low, capacity)
        ]
    return states[-1]


def solution(mesh):
    placed = (
        P("seq"),
        P("seq", "table"),
        P(),
        P(),
        P("table", None, None, "seq", None),
        P(),
        P(),
        P(),
        P(),
    )
    return jax.shard_map(
        local, mesh=mesh, in_specs=placed, out_specs=P(("table", "seq"), None), check_vma=False
    )
```

time: 97.2 us -> 87.3 us (0.90)
  Pallas kernels: 67.9 us -> 52.8 us
  waiting for transfers between devices: 6.78 us -> 16 us
  local copies, waits for them, and re-layouts: 4.55 us -> 1.7 us
  starting transfers between devices: 17.2 us -> 16.2 us
    pallas_call x5 -> x3, Pallas kernels: 67.9 us -> 52.8 us  [the longest x2 38.5 us: rank(): pl.pallas_call(functools.partial(rank_kernel, low, capacity, done, shards...]
    ppermute x6, waiting for transfers between devices: 0.02 us -> 5.01 us  [gather_history(): lax.ppermute(v, 'seq', route)]
    all_to_all x2, waiting for transfers between devices: 6.76 us -> 11 us  [local(): lax.all_to_all(chunk, 'table', split_axis=0, concat_axis=0, tiled=True)]
    unnamed x8 -> x18, local copies, waits for them, and re-layouts: 3.49 us -> 1.66 us
    squeeze x1, local copies, waits for them, and re-layouts: 1.06 us -> 0.04 us  [gather_history(): held = {0: history[0, :, kind]}]
  transfers between devices with their start and end apart: 8 -> 8, of which waited for: 1 -> 2; matrix products, arithmetic and copies ran while one was open for 0% -> 0% of each run, Pallas kernels for 51% -> 23%
where the time goes in v1:
time: 87.3 us; the launch traced here: 87 us
  Pallas kernels  52.8 us (60%)
  starting transfers between devices  16.2 us (19%)
  waiting for transfers between devices  16 us (18%)
  local copies, waits for them, and re-layouts  1.7 us (2%)
    pallas_call x2, Pallas kernels, rank(): pl.pallas_call(functools.partial(rank_kernel, low, capacity, done, shards...  38.5 us
    pallas_call x1, Pallas kernels, lookup(): pl.pallas_call(functools.partial(lookup_kernel, cuts), out_shape=tuple((j...  14.3 us
    all_to_all x2, waiting for transfers between devices, local(): lax.all_to_all(chunk, 'table', split_axis=0, concat_axis=0, tiled=True)  11 us
    all_to_all x2, starting transfers between devices, local(): lax.all_to_all(chunk, 'table', split_axis=0, concat_axis=0, tiled=True)  10.7 us
    ppermute x6, starting transfers between devices, gather_history(): lax.ppermute(v, 'seq', route)  5.45 us
    ppermute x6, waiting for transfers between devices, gather_history(): lax.ppermute(v, 'seq', route)  5.01 us
  transfers between devices with their start and end apart: 8, of which 2 were waited for; matrix products, arithmetic and copies ran while one was open for 0% of the time, Pallas kernels for 23%

profile of v1, /device:TPU:1, one launch (start us, length us, event | category | flops | bytes accessed | tf_op | source)
XLA Modules:
  0.0 87.0 jit_solution(16514982108290821367)
XLA Ops:
  0.0 0.0 copy-start.2
  0.0 14.3 %lookup.1 = (bf16[8,416,128]{2,1,0:T(8,128)(2,1)}, bf16[8,352,128]{2,1,0:T(8,128)(2,1)}) custom-call(s32[8192]{0:T(1024)} %ids.1, s32[8,4,8]{2,1,0:T(4,128)} %counts.5, bf16[64,32768]{1,0:T(8,128)(2,1)} %bitcast.9), custom_call_target="tpu_custom_call" | custom-call | tf_op jit(solution)/shard_map/lookup/pallas_call | solution.py:104
  14.3 6.4 %all-to-all-start.1 = ((bf16[8,416,128]{2,1,0:T(8,128)(2,1)}), bf16[8,416,128]{2,1,0:T(8,128)(2,1)S(1)}, u32[]{:S(2)}, u32[]{:S(2)}) async-start(bf16[8,416,128]{2,1,0:T(8,128)(2,1)} %get-tuple-element.8), calls=%async_computation.1 | async-start | bytes 1703936 | tf_op jit(solution)/shard_map/all_to_all | solution.py:345
  20.7 0.0 copy-done.2
  20.7 0.0 copy-start.4
  20.7 0.0 copy-start.3
  20.7 1.3 %collective-permute-start.4 = (bf16[2,128,512]{2,1,0:T(8,128)(2,1)S(1)}, bf16[2,128,512]{2,1,0:T(8,128)(2,1)S(1)}, u32[]{:S(2)}, u32[]{:S(2)}) collective-permute-start(bf16[2,128,512]{2,1,0:T(8,128)(2,1)S(1)} %get-tuple-element.9.refs_4_.refs_5_), channel_id=1, source_target_pairs={{0,2},{1,3},{2,0},{3,1},{4,6},{5,7},{6,4},{7,5},{8,10},{9,11},{10,... | collective-permute-start | bytes 786440 | tf_op jit(solution)/shard_map/ppermute | solution.py:135
  22.1 1.2 %collective-permute-start = (bf16[2,128,512]{2,1,0:T(8,128)(2,1)S(1)}, bf16[2,128,512]{2,1,0:T(8,128)(2,1)S(1)}, u32[]{:S(2)}, u32[]{:S(2)}) collective-permute-start(bf16[2,128,512]{2,1,0:T(8,128)(2,1)S(1)} %get-tuple-element.10.refs_0_.refs_1_), channel_id=1, source_target_pairs={{0,1},{1,0},{2,3},{3,2},{4,5},{5,4},{6,7},{7,6},{8,9},{9,8},{10,11... | collective-permute-start | bytes 786440 | tf_op jit(solution)/shard_map/ppermute | solution.py:135
  23.3 0.3 collective-permute-start.3
  23.5 0.2 collective-permute-start.1
  23.7 5.0 %collective-permute-done.4.refs_6_.refs_7_ = bf16[2,128,512]{2,1,0:T(8,128)(2,1)S(1)} collective-permute-done((bf16[2,128,512]{2,1,0:T(8,128)(2,1)S(1)}, bf16[2,128,512]{2,1,0:T(8,128)(2,1)S(1)}, u32[]{:S(2)}, u32[]{:S(2)}) %collective-permute-start.4) | collective-permute-done | bytes 262176 | tf_op jit(solution)/shard_map/ppermute | solution.py:135
  28.7 0.0 copy-start.5
  28.7 1.2 %collective-permute-start.5 = (bf16[2,128,512]{2,1,0:T(8,128)(2,1)S(1)}, bf16[2,128,512]{2,1,0:T(8,128)(2,1)}, u32[]{:S(2)}, u32[]{:S(2)}) collective-permute-start(bf16[2,128,512]{2,1,0:T(8,128)(2,1)S(1)} %collective-permute-done.4.refs_6_.refs_7_), channel_id=1, source_target_pairs={{0,1},{1,0},{2,3},{3,2},{4,5},{5,4},{6,7},{7,6},{8,9},{9,8},{10,11... | collective-permute-start | bytes 786440 | tf_op jit(solution)/shard_map/ppermute | solution.py:135
  30.0 0.0 collective-permute-done.refs_1_.refs_2_
  30.0 0.0 copy-start.6
  30.0 1.2 %collective-permute-start.2 = (bf16[2,128,512]{2,1,0:T(8,128)(2,1)S(1)}, bf16[2,128,512]{2,1,0:T(8,128)(2,1)}, u32[]{:S(2)}, u32[]{:S(2)}) collective-permute-start(bf16[2,128,512]{2,1,0:T(8,128)(2,1)S(1)} %collective-permute-done.refs_1_.refs_2_), channel_id=1, source_target_pairs={{0,2},{1,3},{2,0},{3,1},{4,6},{5,7},{6,4},{7,5},{8,10},{9,11},{10,... | collective-permute-start | bytes 786440 | tf_op jit(solution)/shard_map/ppermute | solution.py:135
  31.2 11.0 %all-to-all-done.1.pieces = bf16[8,416,128]{2,1,0:T(8,128)(2,1)S(1)} async-done(((bf16[8,416,128]{2,1,0:T(8,128)(2,1)}), bf16[8,416,128]{2,1,0:T(8,128)(2,1)S(1)}, u32[]{:S(2)}, u32[]{:S(2)}) %all-to-all-start.1) | async-done | bytes 852000 | tf_op jit(solution)/shard_map/all_to_all | solution.py:345
  42.2 0.0 copy-start
  42.2 4.3 %all-to-all-start = ((bf16[8,352,128]{2,1,0:T(8,128)(2,1)}), bf16[8,352,128]{2,1,0:T(8,128)(2,1)S(1)}, u32[]{:S(2)}, u32[]{:S(2)}) async-start(bf16[8,352,128]{2,1,0:T(8,128)(2,1)} %get-tuple-element.7), calls=%async_computation | async-start | bytes 1441792 | tf_op jit(solution)/shard_map/all_to_all | solution.py:345
  46.5 0.0 collective-permute-done.3.refs_5_.refs_6_
  46.5 0.0 copy-done.4
  46.5 0.0 copy-start.7
  46.5 0.0 collective-permute-done.1.refs_2_.refs_3_
  46.5 0.0 copy-done.5
  46.6 0.0 copy-start.8
  46.6 0.0 collective-permute-done.5.refs_7_.refs_8_
  46.6 0.0 copy-done.6
  46.6 0.6 copy-done.7
  47.2 0.1 copy-done.8
  47.3 0.0 collective-permute-done.2.refs_3_.refs_4_
  47.3 0.0 copy-done.3
  47.3 0.0 copy-done
  47.3 20.2 %rank.2.refs_0_ = bf16[832,512]{1,0:T(8,128)(2,1)} custom-call(s32[8,4,8]{2,1,0:T(4,128)} %counts.5, s32[8]{0:T(128)} %lengths.3, bf16[8,416,128]{2,1,0:T(8,128)(2,1)} %copy-done, bf16[2,128,512]{2,1,0:T(8,128)(2,1)} %copy-done.4, bf16[2,128,512]{2,1,0:T(8,128)(2,1)} %copy-done.6, bf16[2,128,512]{2,1,0:T(8,128)(2,1)} %copy-done.8, ...), custom_call_target="tpu_custom_call" | custom-call | flops 20000000000 | bytes 20000000 | tf_op jit(solution)/shard_map/rank/pallas_call | solution.py:322
  67.6 0.0 all-to-all-done.pieces
  67.6 0.0 copy-start.1
  67.6 0.9 %copy-done.1 = bf16[8,352,128]{2,1,0:T(8,128)(2,1)} copy-done((bf16[8,352,128]{2,1,0:T(8,128)(2,1)}, bf16[8,352,128]{2,1,0:T(8,128)(2,1)S(1)}, u32[]{:S(2)}) %copy-start.1) | copy-done | bytes 720920
  68.5 18.3 %rank.3 = bf16[1536,512]{1,0:T(8,128)(2,1)} custom-call(s32[8,4,8]{2,1,0:T(4,128)} %counts.5, s32[8]{0:T(128)} %lengths.3, bf16[8,352,128]{2,1,0:T(8,128)(2,1)} %copy-done.1, bf16[832,512]{1,0:T(8,128)(2,1)} %rank.2.refs_0_, bf16[2,128,512]{2,1,0:T(8,128)(2,1)} %copy-done.4, bf16[2,128,512]{2,1,0:T(8,128)(2,1)} %copy-done.6, bf16[2,128,512]{2,1,0:T(8,128)(2,1)} %copy-done.8, ...), custom_call_target="tpu_custom_call" | custom-call | flops 20000000000 | bytes 20000000 | tf_op jit(solution)/shard_map/rank/pallas_call | solution.py:322
  (1 shorter events, 0.0 us)
Async XLA Ops:
  0.0 20.7 %copy-start.2 = (bf16[1,2,2,128,512]{4,3,2,1,0:T(8,128)(2,1)S(1)}, bf16[1,2,2,128,512]{4,3,2,1,0:T(8,128)(2,1)}, u32[]{:S(2)}) copy-start(bf16[1,2,2,128,512]{4,3,2,1,0:T(8,128)(2,1)} %param.13) | copy-start | bytes 1572868
  14.3 27.9 %all-to-all-start.1 = ((bf16[8,416,128]{2,1,0:T(8,128)(2,1)}), bf16[8,416,128]{2,1,0:T(8,128)(2,1)S(1)}, u32[]{:S(2)}, u32[]{:S(2)}) async-start(bf16[8,416,128]{2,1,0:T(8,128)(2,1)} %get-tuple-element.8), calls=%async_computation.1 | async-start | bytes 1703936 | tf_op jit(solution)/shard_map/all_to_all | solution.py:345
  20.7 25.8 %copy-start.4 = (bf16[2,128,512]{2,1,0:T(8,128)(2,1)}, bf16[2,128,512]{2,1,0:T(8,128)(2,1)S(1)}, u32[]{:S(2)}) copy-start(bf16[2,128,512]{2,1,0:T(8,128)(2,1)S(1)} %get-tuple-element.10.refs_0_.refs_1_) | copy-start | bytes 786436
  20.7 26.6 %copy-start.3 = (bf16[2,128,512]{2,1,0:T(8,128)(2,1)}, bf16[2,128,512]{2,1,0:T(8,128)(2,1)S(1)}, u32[]{:S(2)}) copy-start(bf16[2,128,512]{2,1,0:T(8,128)(2,1)S(1)} %get-tuple-element.9.refs_4_.refs_5_) | copy-start | bytes 786436
  20.7 8.0 %collective-permute-start.4 = (bf16[2,128,512]{2,1,0:T(8,128)(2,1)S(1)}, bf16[2,128,512]{2,1,0:T(8,128)(2,1)S(1)}, u32[]{:S(2)}, u32[]{:S(2)}) collective-permute-start(bf16[2,128,512]{2,1,0:T(8,128)(2,1)S(1)} %get-tuple-element.9.refs_4_.refs_5_), channel_id=1, source_target_pairs={{0,2},{1,3},{2,0},{3,1},{4,6},{5,7},{6,4},{7,5},{8,10},{9,11},{10,... | collective-permute-start | bytes 786440 | tf_op jit(solution)/shard_map/ppermute | solution.py:135
  22.1 7.9 %collective-permute-start = (bf16[2,128,512]{2,1,0:T(8,128)(2,1)S(1)}, bf16[2,128,512]{2,1,0:T(8,128)(2,1)S(1)}, u32[]{:S(2)}, u32[]{:S(2)}) collective-permute-start(bf16[2,128,512]{2,1,0:T(8,128)(2,1)S(1)} %get-tuple-element.10.refs_0_.refs_1_), channel_id=1, source_target_pairs={{0,1},{1,0},{2,3},{3,2},{4,5},{5,4},{6,7},{7,6},{8,9},{9,8},{10,11... | collective-permute-start | bytes 786440 | tf_op jit(solution)/shard_map/ppermute | solution.py:135
  23.3 23.3 %collective-permute-start.3 = (bf16[2,128,512]{2,1,0:T(8,128)(2,1)S(1)}, bf16[2,128,512]{2,1,0:T(8,128)(2,1)S(1)}, u32[]{:S(2)}, u32[]{:S(2)}) collective-permute-start(bf16[2,128,512]{2,1,0:T(8,128)(2,1)S(1)} %get-tuple-element.9.refs_4_.refs_5_), channel_id=1, source_target_pairs={{0,1},{1,0},{2,3},{3,2},{4,5},{5,4},{6,7},{7,6},{8,9},{9,8},{10,11... | collective-permute-start | bytes 786440 | tf_op jit(solution)/shard_map/ppermute | solution.py:135
  23.5 23.0 %collective-permute-start.1 = (bf16[2,128,512]{2,1,0:T(8,128)(2,1)S(1)}, bf16[2,128,512]{2,1,0:T(8,128)(2,1)S(1)}, u32[]{:S(2)}, u32[]{:S(2)}) collective-permute-start(bf16[2,128,512]{2,1,0:T(8,128)(2,1)S(1)} %get-tuple-element.10.refs_0_.refs_1_), channel_id=1, source_target_pairs={{0,2},{1,3},{2,0},{3,1},{4,6},{5,7},{6,4},{7,5},{8,10},{9,11},{10,... | collective-permute-start | bytes 786440 | tf_op jit(solution)/shard_map/ppermute | solution.py:135
  28.7 17.8 %copy-start.5 = (bf16[2,128,512]{2,1,0:T(8,128)(2,1)}, bf16[2,128,512]{2,1,0:T(8,128)(2,1)S(1)}, u32[]{:S(2)}) copy-start(bf16[2,128,512]{2,1,0:T(8,128)(2,1)S(1)} %collective-permute-done.4.refs_6_.refs_7_) | copy-start | bytes 786436
  28.7 17.8 %collective-permute-start.5 = (bf16[2,128,512]{2,1,0:T(8,128)(2,1)S(1)}, bf16[2,128,512]{2,1,0:T(8,128)(2,1)}, u32[]{:S(2)}, u32[]{:S(2)}) collective-permute-start(bf16[2,128,512]{2,1,0:T(8,128)(2,1)S(1)} %collective-permute-done.4.refs_6_.refs_7_), channel_id=1, source_target_pairs={{0,1},{1,0},{2,3},{3,2},{4,5},{5,4},{6,7},{7,6},{8,9},{9,8},{10,11... | collective-permute-start | bytes 786440 | tf_op jit(solution)/shard_map/ppermute | solution.py:135
  30.0 16.6 %copy-start.6 = (bf16[2,128,512]{2,1,0:T(8,128)(2,1)}, bf16[2,128,512]{2,1,0:T(8,128)(2,1)S(1)}, u32[]{:S(2)}) copy-start(bf16[2,128,512]{2,1,0:T(8,128)(2,1)S(1)} %collective-permute-done.refs_1_.refs_2_) | copy-start | bytes 786436
  30.0 17.4 %collective-permute-start.2 = (bf16[2,128,512]{2,1,0:T(8,128)(2,1)S(1)}, bf16[2,128,512]{2,1,0:T(8,128)(2,1)}, u32[]{:S(2)}, u32[]{:S(2)}) collective-permute-start(bf16[2,128,512]{2,1,0:T(8,128)(2,1)S(1)} %collective-permute-done.refs_1_.refs_2_), channel_id=1, source_target_pairs={{0,2},{1,3},{2,0},{3,1},{4,6},{5,7},{6,4},{7,5},{8,10},{9,11},{10,... | collective-permute-start | bytes 786440 | tf_op jit(solution)/shard_map/ppermute | solution.py:135
  42.2 5.1 %copy-start = (bf16[8,416,128]{2,1,0:T(8,128)(2,1)}, bf16[8,416,128]{2,1,0:T(8,128)(2,1)S(1)}, u32[]{:S(2)}) copy-start(bf16[8,416,128]{2,1,0:T(8,128)(2,1)S(1)} %all-to-all-done.1.pieces) | copy-start | bytes 2555908
  42.2 25.4 %all-to-all-start = ((bf16[8,352,128]{2,1,0:T(8,128)(2,1)}), bf16[8,352,128]{2,1,0:T(8,128)(2,1)S(1)}, u32[]{:S(2)}, u32[]{:S(2)}) async-start(bf16[8,352,128]{2,1,0:T(8,128)(2,1)} %get-tuple-element.7), calls=%async_computation | async-start | bytes 1441792 | tf_op jit(solution)/shard_map/all_to_all | solution.py:345
  46.5 0.7 copy-start.7
  46.6 0.8 copy-start.8
  67.6 0.9 %copy-start.1 = (bf16[8,352,128]{2,1,0:T(8,128)(2,1)}, bf16[8,352,128]{2,1,0:T(8,128)(2,1)S(1)}, u32[]{:S(2)}) copy-start(bf16[8,352,128]{2,1,0:T(8,128)(2,1)S(1)} %all-to-all-done.pieces) | copy-start | bytes 2162692

commit v2 on v1

--- a/solution.py
+++ b/solution.py
@@ -9,7 +9,7 @@
 
 HEADS = 8
 LANES = 128
-UNROLL = 64
+UNROLL = 256
 MIB = 1 << 20
 ANY = pl.BlockSpec(memory_space=pl.ANY)
 SMEM = pl.BlockSpec(memory_space=pltpu.SMEM)
@@ -46,18 +46,11 @@
     id_vector[...] = id_vector[...] - shard * vocab
     put_ids = pltpu.make_async_copy(id_vector, local_ids, sems.at[2])
     put_ids.start()
-    inner = 1024
     for part in range(parts):
         get_table[part].wait()
-
-        def turn(step, carry, part=part):
-            at = pl.multiple_of(part * block + step * inner, inner)
-            piece = table[:, pl.ds(at, inner)]
-            piece = jnp.concatenate([piece] * packing, axis=0)
-            rows_major[pl.ds(at, inner), :] = piece.T.astype(jnp.float32)
-            return carry
-
-        lax.fori_loop(0, block // inner, turn, 0)
+        piece = table[:, part * block : (part + 1) * block]
+        piece = jnp.concatenate([piece] * packing, axis=0)
+        rows_major[pl.ds(part * block, block), :] = piece.T.astype(jnp.float32)
     get_counts.wait()
     put_ids.wait()
 
@@ -119,7 +112,7 @@
             pltpu.SMEM(counts.shape, jnp.int32),
             pltpu.SemaphoreType.DMA((11,)),
         ],
-        compiler_params=pltpu.CompilerParams(vmem_limit_bytes=62 * MIB),
+        compiler_params=pltpu.CompilerParams(vmem_limit_bytes=64 * MIB - MIB // 4),
         name="lookup",
     )(ids, counts, table_t)
 
@@ -151,19 +144,23 @@
     )
 
 
-def row_mean(values):
-    width = values.shape[1]
-    partial = sum(values[:, at : at + LANES] for at in range(0, width, LANES))
+def row_mean(blocks):
+    partial = sum(blocks[1:], blocks[0])
     high = partial.astype(jnp.bfloat16)
     low = (partial - high.astype(jnp.float32)).astype(jnp.bfloat16)
-    ones = jnp.full((2 * LANES, LANES), 1.0 / width, jnp.bfloat16)
-    mean = dot(jnp.concatenate([high, low], axis=1), ones)
-    return jnp.concatenate([mean] * (width // LANES), axis=1)
-
-
-def normalized(values):
-    centred = values - row_mean(values)
-    return centred * lax.rsqrt(row_mean(centred * centred) + 1e-06)
+    ones = jnp.full((2 * LANES, LANES), 1.0 / (LANES * len(blocks)), jnp.bfloat16)
+    return dot(jnp.concatenate([high, low], axis=1), ones)
+
+
+def normalized(blocks):
+    mean = row_mean(blocks)
+    centred = [block - mean for block in blocks]
+    factor = lax.rsqrt(row_mean([block * block for block in centred]) + 1e-06)
+    return [block * factor for block in centred]
+
+
+def in_blocks(values):
+    return [values[:, at : at + LANES] for at in range(0, values.shape[1], LANES)]
 
 
 def rank_kernel(low, capacity, done, shards, counts, lengths, pieces, *refs):
@@ -171,7 +168,8 @@
     history, refs = refs[: 2 * shards], refs[2 * shards :]
     weights, out, refs = refs[:4], refs[4], refs[5:]
     ranked, refs = (refs[0], refs[1:]) if done else (None, refs)
-    keys, values, w_in, w_out, w_proj, w_back, sems = refs
+    got, keys, values, w_in, w_out, w_proj, w_back, sems, refs = *refs[:8], refs[8:]
+    pieces_in_hbm, pieces = pieces, got
     groups, part, _ = pieces.shape
     width = w_in.shape[0]
     packing = groups * LANES // width
@@ -183,6 +181,12 @@
         0, groups, lambda t, n: n + counts[t, shard, table_index], jnp.int32(0)
     )
 
+    get_pieces = pltpu.make_async_copy(pieces_in_hbm, pieces, sems.at[sems.shape[0] - 1])
+    get_before = []
+    for k, piece in enumerate(before):
+        get_before.append(pltpu.make_async_copy(piece, refs[k], sems.at[sems.shape[0] - 2 - k]))
+        get_before[-1].start()
+
     def keep(states):
         if done:
             for block in range(width // LANES):
@@ -193,13 +197,40 @@
             out[...] = states
 
     if done:
+        slots, put_sems = refs[done], refs[done + 1]
+        slot_row = lax.broadcasted_iota(jnp.int32, (capacity, LANES), 0)
+
+    def put(sender):
+        place = pl.ds(pl.multiple_of(sender * capacity, capacity), capacity)
+        return pltpu.make_async_copy(slots.at[place], out.at[place], put_sems.at[sender])
+
+    def fill_before():
         at = 0
-        for piece in before:
+        for copy, piece in zip(get_before, refs):
+            copy.wait()
             for block in range(width // LANES):
                 ranked[block, pl.ds(at, piece.shape[0]), :] = piece[
                     :, pl.ds(block * LANES, LANES)
                 ].astype(jnp.float32)
             at += piece.shape[0]
+
+    def fill_slots(early):
+        def slot_block(sender, start):
+            amount = counts[sender, shard, table_index]
+
+            @pl.when((start + amount <= low) == early)
+            def _():
+                for block in range(width // LANES):
+                    value = ranked[block, pl.ds(start, capacity), :]
+                    slots[
+                        pl.ds(pl.multiple_of(sender * capacity, capacity), capacity),
+                        block * LANES : (block + 1) * LANES,
+                    ] = jnp.where(slot_row < amount, value, 0.0).astype(jnp.bfloat16)
+                put(sender).start()
+
+            return start + amount
+
+        lax.fori_loop(0, groups, slot_block, jnp.int32(0))
 
     @pl.when(low < filled)
     def _():
@@ -222,8 +253,14 @@
             pltpu.make_async_copy(source, target, sems.at[k])
             for k, (source, target) in enumerate(views)
         ]
-        for copy in copies[:4]:
+        copies[0].start()
+        get_pieces.start()
+        for copy in copies[1:4]:
             copy.start()
+        if done:
+            fill_before()
+            fill_slots(True)
+        get_pieces.wait()
         lane = lax.broadcasted_iota(jnp.int32, (part, LANES), 1) // columns
         row = lax.broadcasted_iota(jnp.int32, (part, LANES), 0)
         rows = []
@@ -263,7 +300,13 @@
         first = lax.broadcasted_iota(jnp.int32, (tile, pair), 1) < pair // 2
         scale = 0.5 * (width // HEADS) ** -0.5
         for layer in range(w_proj.shape[0]):
-            normed = normalized(states.astype(jnp.float32)).astype(jnp.bfloat16)
+            normed = jnp.concatenate(
+                [
+                    block.astype(jnp.bfloat16)
+                    for block in normalized(in_blocks(states.astype(jnp.float32)))
+                ],
+                axis=1,
+            )
             queries = half_silu(dot(normed, w_proj[layer, :, width:]) * 0.5) * scale
             queries = queries.astype(jnp.bfloat16)
             kept = jnp.where(cached, keys[layer], jnp.zeros((), jnp.bfloat16))
@@ -284,26 +327,25 @@
                 both = dot(weighted, values[layer, :, block * pair : (block + 1) * pair])
                 attended.append(jnp.where(first, both[:tile], both[tile:]))
                 scores = following
-            attended = jnp.concatenate(attended, axis=1)
             gate = half_silu(dot(normed, w_proj[layer, :, :width]) * 0.5)
-            mixed = (normalized(attended) * gate).astype(jnp.bfloat16)
+            mixed = [
+                (block * open_).astype(jnp.bfloat16)
+                for block, open_ in zip(normalized(attended), in_blocks(gate))
+            ]
+            mixed = jnp.concatenate(mixed, axis=1)
             states = (states.astype(jnp.float32) + dot(mixed, w_back[layer])).astype(jnp.bfloat16)
         keep(states)
 
     if done:
-        row = lax.broadcasted_iota(jnp.int32, (capacity, LANES), 0)
-
-        def slot_block(sender, start):
-            amount = counts[sender, shard, table_index]
-            for block in range(width // LANES):
-                value = ranked[block, pl.ds(start, capacity), :]
-                out[
-                    pl.ds(pl.multiple_of(sender * capacity, capacity), capacity),
-                    block * LANES : (block + 1) * LANES,
-                ] = jnp.where(row < amount, value, 0.0).astype(jnp.bfloat16)
-            return start + amount
-
-        lax.fori_loop(0, groups, slot_block, jnp.int32(0))
+
+        @pl.when(low >= filled)
+        def _():
+            fill_before()
+            fill_slots(True)
+
+        fill_slots(False)
+        for sender in range(groups):
+            put(sender).wait()
 
 
 def rank(counts, lengths, pieces, before, history, weights, low, capacity):
@@ -314,18 +356,21 @@
     done = len(before)
     layers, piece_rows, _ = history[0].shape
     shards = len(history) // 2
-    scratch = [pltpu.VMEM((layers, shards * piece_rows, width), jnp.bfloat16)] * 2
+    scratch = [pltpu.VMEM(pieces.shape, pieces.dtype)]
+    scratch += [pltpu.VMEM((layers, shards * piece_rows, width), jnp.bfloat16)] * 2
     scratch += [pltpu.VMEM(weight.shape, weight.dtype) for weight in weights]
-    scratch += [pltpu.SemaphoreType.DMA((len(weights) + 2 + len(history),))]
+    scratch += [pltpu.SemaphoreType.DMA((len(weights) + 3 + len(history) + done,))]
     if done:
         scratch = [pltpu.VMEM((width // LANES, total + capacity, LANES), jnp.float32)] + scratch
+        scratch += [pltpu.VMEM(piece.shape, piece.dtype) for piece in before]
+        scratch += [pltpu.VMEM((total, width), jnp.bfloat16), pltpu.SemaphoreType.DMA((groups,))]
     return pl.pallas_call(
         functools.partial(rank_kernel, low, capacity, done, shards),
         out_shape=jax.ShapeDtypeStruct((total if done else tile, width), jnp.bfloat16),
-        in_specs=[SMEM, SMEM, VMEM] + [VMEM] * done + [ANY] * (len(history) + len(weights)),
-        out_specs=VMEM,
+        in_specs=[SMEM, SMEM] + [ANY] * (1 + done + len(history) + len(weights)),
+        out_specs=ANY if done else VMEM,
         scratch_shapes=scratch,
-        compiler_params=pltpu.CompilerParams(vmem_limit_bytes=62 * MIB),
+        compiler_params=pltpu.CompilerParams(vmem_limit_bytes=64 * MIB - MIB // 4),
         cost_estimate=pl.CostEstimate(
             flops=20_000_000_000, bytes_accessed=20_000_000, transcendentals=0
         ),
@@ -338,7 +383,7 @@
     row_count = item_ids.shape[0] // groups
     capacity = 3 * row_count // (2 * groups)
     total = groups * capacity
-    cuts = (0, total * 13 // 24, total)
+    cuts = (0, total // 2, total)
     table_t = item_table.T
     found = lookup(item_ids, group_counts, table_t, cuts)
     pieces = [

time: 87.3 us -> 85.5 us (0.979)
  waiting for transfers between devices: 16 us -> 13.5 us
  Pallas kernels: 52.8 us -> 51.7 us
    all_to_all x2, waiting for transfers between devices: 11 us -> 8.56 us  [local(): lax.all_to_all(chunk, 'table', split_axis=0, concat_axis=0, tiled=True)]
    pallas_call x1, Pallas kernels: 14.3 us -> 12.4 us  [lookup(): pl.pallas_call(functools.partial(lookup_kernel, cuts), out_shape=tuple((j...]
    squeeze x1, local copies, waits for them, and re-layouts: 0.04 us -> 1.06 us  [gather_history(): held = {0: history[0, :, kind]}]
  transfers between devices with their start and end apart: 8 -> 8, of which waited for: 2 -> 2; matrix products, arithmetic and copies ran while one was open for 0% -> 1% of each run, Pallas kernels for 23% -> 23%
where the time goes in v2:
time: 85.5 us; the launch traced here: 85 us
  Pallas kernels  51.7 us (60%)
  starting transfers between devices  16.9 us (20%)
  waiting for transfers between devices  13.5 us (16%)
  local copies, waits for them, and re-layouts  2.52 us (3%)
    pallas_call x2, Pallas kernels, rank(): pl.pallas_call(functools.partial(rank_kernel, low, capacity, done, shards...  39.3 us
    pallas_call x1, Pallas kernels, lookup(): pl.pallas_call(functools.partial(lookup_kernel, cuts), out_shape=tuple((j...  12.4 us
    all_to_all x2, starting transfers between devices, local(): lax.all_to_all(chunk, 'table', split_axis=0, concat_axis=0, tiled=True)  11.3 us
    all_to_all x2, waiting for transfers between devices, local(): lax.all_to_all(chunk, 'table', split_axis=0, concat_axis=0, tiled=True)  8.56 us
    ppermute x6, starting transfers between devices, gather_history(): lax.ppermute(v, 'seq', route)  5.59 us
    ppermute x6, waiting for transfers between devices, gather_history(): lax.ppermute(v, 'seq', route)  4.98 us
  transfers between devices with their start and end apart: 8, of which 2 were waited for; matrix products, arithmetic and copies ran while one was open for 1% of the time, Pallas kernels for 23%

profile of v2, /device:TPU:1, one launch (start us, length us, event | category | flops | bytes accessed | tf_op | source)
XLA Modules:
  0.0 85.0 jit_solution(13993206247609973516)
XLA Ops:
  0.0 12.4 %lookup.1 = (bf16[8,384,128]{2,1,0:T(8,128)(2,1)}, bf16[8,384,128]{2,1,0:T(8,128)(2,1)}) custom-call(s32[8192]{0:T(1024)} %ids.1, s32[8,4,8]{2,1,0:T(4,128)} %counts.5, bf16[64,32768]{1,0:T(8,128)(2,1)} %bitcast.9), custom_call_target="tpu_custom_call" | custom-call | tf_op jit(solution)/shard_map/lookup/pallas_call | solution.py:97
  12.4 6.4 %all-to-all-start.1 = ((bf16[8,384,128]{2,1,0:T(8,128)(2,1)}), bf16[8,384,128]{2,1,0:T(8,128)(2,1)}, u32[]{:S(2)}, u32[]{:S(2)}) async-start(bf16[8,384,128]{2,1,0:T(8,128)(2,1)} %get-tuple-element.8), calls=%async_computation.1 | async-start | bytes 1572864 | tf_op jit(solution)/shard_map/all_to_all | solution.py:390
  18.8 1.1 %slice_bitcast_fusion = (bf16[2,128,512]{2,1,0:T(8,128)(2,1)S(1)}, bf16[2,128,512]{2,1,0:T(8,128)(2,1)S(1)}) fusion(bf16[1,2,2,128,512]{4,3,2,1,0:T(8,128)(2,1)} %param.13), kind=kLoop, calls=%fused_computation | loop fusion | bytes 1048576 | tf_op jit(solution)/shard_map/squeeze | solution.py:125
  19.8 0.0 copy-start
  19.9 0.0 copy-start.1
  19.9 1.3 %collective-permute-start.4 = (bf16[2,128,512]{2,1,0:T(8,128)(2,1)S(1)}, bf16[2,128,512]{2,1,0:T(8,128)(2,1)S(1)}, u32[]{:S(2)}, u32[]{:S(2)}) collective-permute-start(bf16[2,128,512]{2,1,0:T(8,128)(2,1)S(1)} %get-tuple-element.9.refs_4_.refs_5_), channel_id=1, source_target_pairs={{0,2},{1,3},{2,0},{3,1},{4,6},{5,7},{6,4},{7,5},{8,10},{9,11},{10,... | collective-permute-start | bytes 786440 | tf_op jit(solution)/shard_map/ppermute | solution.py:128
  21.2 1.2 %collective-permute-start = (bf16[2,128,512]{2,1,0:T(8,128)(2,1)S(1)}, bf16[2,128,512]{2,1,0:T(8,128)(2,1)S(1)}, u32[]{:S(2)}, u32[]{:S(2)}) collective-permute-start(bf16[2,128,512]{2,1,0:T(8,128)(2,1)S(1)} %get-tuple-element.10.refs_0_.refs_1_), channel_id=1, source_target_pairs={{0,1},{1,0},{2,3},{3,2},{4,5},{5,4},{6,7},{7,6},{8,9},{9,8},{10,11... | collective-permute-start | bytes 786440 | tf_op jit(solution)/shard_map/ppermute | solution.py:128
  22.4 0.0 copy-done
  22.4 0.3 collective-permute-start.3
  22.6 0.4 collective-permute-start.1
  23.0 5.0 %collective-permute-done.4.refs_6_.refs_7_ = bf16[2,128,512]{2,1,0:T(8,128)(2,1)S(1)} collective-permute-done((bf16[2,128,512]{2,1,0:T(8,128)(2,1)S(1)}, bf16[2,128,512]{2,1,0:T(8,128)(2,1)S(1)}, u32[]{:S(2)}, u32[]{:S(2)}) %collective-permute-start.4) | collective-permute-done | bytes 262176 | tf_op jit(solution)/shard_map/ppermute | solution.py:128
  28.0 0.0 copy-start.2
  28.0 1.2 %collective-permute-start.5 = (bf16[2,128,512]{2,1,0:T(8,128)(2,1)S(1)}, bf16[2,128,512]{2,1,0:T(8,128)(2,1)S(1)}, u32[]{:S(2)}, u32[]{:S(2)}) collective-permute-start(bf16[2,128,512]{2,1,0:T(8,128)(2,1)S(1)} %collective-permute-done.4.refs_6_.refs_7_), channel_id=1, source_target_pairs={{0,1},{1,0},{2,3},{3,2},{4,5},{5,4},{6,7},{7,6},{8,9},{9,8},{10,11... | collective-permute-start | bytes 786440 | tf_op jit(solution)/shard_map/ppermute | solution.py:128
  29.2 0.0 collective-permute-done.refs_1_.refs_2_
  29.2 0.0 copy-start.3
  29.2 1.2 %collective-permute-start.2 = (bf16[2,128,512]{2,1,0:T(8,128)(2,1)S(1)}, bf16[2,128,512]{2,1,0:T(8,128)(2,1)}, u32[]{:S(2)}, u32[]{:S(2)}) collective-permute-start(bf16[2,128,512]{2,1,0:T(8,128)(2,1)S(1)} %collective-permute-done.refs_1_.refs_2_), channel_id=1, source_target_pairs={{0,2},{1,3},{2,0},{3,1},{4,6},{5,7},{6,4},{7,5},{8,10},{9,11},{10,... | collective-permute-start | bytes 786440 | tf_op jit(solution)/shard_map/ppermute | solution.py:128
  30.4 8.6 %all-to-all-done.1.pieces = bf16[8,384,128]{2,1,0:T(8,128)(2,1)} async-done(((bf16[8,384,128]{2,1,0:T(8,128)(2,1)}), bf16[8,384,128]{2,1,0:T(8,128)(2,1)}, u32[]{:S(2)}, u32[]{:S(2)}) %all-to-all-start.1) | async-done | bytes 786464 | tf_op jit(solution)/shard_map/all_to_all | solution.py:390
  39.0 5.0 %all-to-all-start = ((bf16[8,384,128]{2,1,0:T(8,128)(2,1)}), bf16[8,384,128]{2,1,0:T(8,128)(2,1)}, u32[]{:S(2)}, u32[]{:S(2)}) async-start(bf16[8,384,128]{2,1,0:T(8,128)(2,1)} %get-tuple-element.7), calls=%async_computation | async-start | bytes 1572864 | tf_op jit(solution)/shard_map/all_to_all | solution.py:390
  44.0 0.0 collective-permute-done.3.refs_5_.refs_6_
  44.0 0.0 copy-done.1
  44.0 0.0 copy-start.4
  44.0 0.0 collective-permute-done.1.refs_2_.refs_3_
  44.0 0.0 copy-done.2
  44.0 0.0 copy-start.5
  44.0 0.0 collective-permute-done.5.refs_7_.refs_8_
  44.0 0.0 copy-done.3
  44.0 0.6 copy-done.4
  44.7 0.1 copy-done.5
  44.8 0.0 copy-start.6
  44.8 0.7 copy-done.6
  45.5 0.0 collective-permute-done.2.refs_3_.refs_4_
  45.5 19.4 %rank.2.refs_0_ = bf16[768,512]{1,0:T(8,128)(2,1)} custom-call(s32[8,4,8]{2,1,0:T(4,128)} %counts.5, s32[8]{0:T(128)} %lengths.3, bf16[8,384,128]{2,1,0:T(8,128)(2,1)} %all-to-all-done.1.pieces, bf16[2,128,512]{2,1,0:T(8,128)(2,1)} %copy-done.1, bf16[2,128,512]{2,1,0:T(8,128)(2,1)} %copy-done.3, bf16[2,128,512]{2,1,0:T(8,128)(2,1)} %copy-done.5, ...), custom_call_target="tpu_custom_call" | custom-call | flops 20000000000 | bytes 20000000 | tf_op jit(solution)/shard_map/rank/pallas_call | solution.py:367
  64.9 0.0 all-to-all-done.pieces
  64.9 19.9 %rank.3 = bf16[1536,512]{1,0:T(8,128)(2,1)} custom-call(s32[8,4,8]{2,1,0:T(4,128)} %counts.5, s32[8]{0:T(128)} %lengths.3, bf16[8,384,128]{2,1,0:T(8,128)(2,1)} %all-to-all-done.pieces, bf16[768,512]{1,0:T(8,128)(2,1)} %rank.2.refs_0_, bf16[2,128,512]{2,1,0:T(8,128)(2,1)} %copy-done.1, bf16[2,128,512]{2,1,0:T(8,128)(2,1)} %copy-done.3, ...), custom_call_target="tpu_custom_call" | custom-call | flops 20000000000 | bytes 20000000 | tf_op jit(solution)/shard_map/rank/pallas_call | solution.py:367
Async XLA Ops:
  12.4 26.6 %all-to-all-start.1 = ((bf16[8,384,128]{2,1,0:T(8,128)(2,1)}), bf16[8,384,128]{2,1,0:T(8,128)(2,1)}, u32[]{:S(2)}, u32[]{:S(2)}) async-start(bf16[8,384,128]{2,1,0:T(8,128)(2,1)} %get-tuple-element.8), calls=%async_computation.1 | async-start | bytes 1572864 | tf_op jit(solution)/shard_map/all_to_all | solution.py:390
  19.8 2.5 %copy-start = (bf16[2,128,512]{2,1,0:T(8,128)(2,1)}, bf16[2,128,512]{2,1,0:T(8,128)(2,1)S(1)}, u32[]{:S(2)}) copy-start(bf16[2,128,512]{2,1,0:T(8,128)(2,1)S(1)} %get-tuple-element.9.refs_4_.refs_5_) | copy-start | bytes 786436
  19.9 24.1 %copy-start.1 = (bf16[2,128,512]{2,1,0:T(8,128)(2,1)}, bf16[2,128,512]{2,1,0:T(8,128)(2,1)S(1)}, u32[]{:S(2)}) copy-start(bf16[2,128,512]{2,1,0:T(8,128)(2,1)S(1)} %get-tuple-element.10.refs_0_.refs_1_) | copy-start | bytes 786436
  19.9 8.1 %collective-permute-start.4 = (bf16[2,128,512]{2,1,0:T(8,128)(2,1)S(1)}, bf16[2,128,512]{2,1,0:T(8,128)(2,1)S(1)}, u32[]{:S(2)}, u32[]{:S(2)}) collective-permute-start(bf16[2,128,512]{2,1,0:T(8,128)(2,1)S(1)} %get-tuple-element.9.refs_4_.refs_5_), channel_id=1, source_target_pairs={{0,2},{1,3},{2,0},{3,1},{4,6},{5,7},{6,4},{7,5},{8,10},{9,11},{10,... | collective-permute-start | bytes 786440 | tf_op jit(solution)/shard_map/ppermute | solution.py:128
  21.2 8.0 %collective-permute-start = (bf16[2,128,512]{2,1,0:T(8,128)(2,1)S(1)}, bf16[2,128,512]{2,1,0:T(8,128)(2,1)S(1)}, u32[]{:S(2)}, u32[]{:S(2)}) collective-permute-start(bf16[2,128,512]{2,1,0:T(8,128)(2,1)S(1)} %get-tuple-element.10.refs_0_.refs_1_), channel_id=1, source_target_pairs={{0,1},{1,0},{2,3},{3,2},{4,5},{5,4},{6,7},{7,6},{8,9},{9,8},{10,11... | collective-permute-start | bytes 786440 | tf_op jit(solution)/shard_map/ppermute | solution.py:128
  22.4 21.6 %collective-permute-start.3 = (bf16[2,128,512]{2,1,0:T(8,128)(2,1)S(1)}, bf16[2,128,512]{2,1,0:T(8,128)(2,1)S(1)}, u32[]{:S(2)}, u32[]{:S(2)}) collective-permute-start(bf16[2,128,512]{2,1,0:T(8,128)(2,1)S(1)} %get-tuple-element.9.refs_4_.refs_5_), channel_id=1, source_target_pairs={{0,1},{1,0},{2,3},{3,2},{4,5},{5,4},{6,7},{7,6},{8,9},{9,8},{10,11... | collective-permute-start | bytes 786440 | tf_op jit(solution)/shard_map/ppermute | solution.py:128
  22.6 21.3 %collective-permute-start.1 = (bf16[2,128,512]{2,1,0:T(8,128)(2,1)S(1)}, bf16[2,128,512]{2,1,0:T(8,128)(2,1)S(1)}, u32[]{:S(2)}, u32[]{:S(2)}) collective-permute-start(bf16[2,128,512]{2,1,0:T(8,128)(2,1)S(1)} %get-tuple-element.10.refs_0_.refs_1_), channel_id=1, source_target_pairs={{0,2},{1,3},{2,0},{3,1},{4,6},{5,7},{6,4},{7,5},{8,10},{9,11},{10,... | collective-permute-start | bytes 786440 | tf_op jit(solution)/shard_map/ppermute | solution.py:128
  28.0 16.0 %copy-start.2 = (bf16[2,128,512]{2,1,0:T(8,128)(2,1)}, bf16[2,128,512]{2,1,0:T(8,128)(2,1)S(1)}, u32[]{:S(2)}) copy-start(bf16[2,128,512]{2,1,0:T(8,128)(2,1)S(1)} %collective-permute-done.4.refs_6_.refs_7_) | copy-start | bytes 786436
  28.0 16.0 %collective-permute-start.5 = (bf16[2,128,512]{2,1,0:T(8,128)(2,1)S(1)}, bf16[2,128,512]{2,1,0:T(8,128)(2,1)S(1)}, u32[]{:S(2)}, u32[]{:S(2)}) collective-permute-start(bf16[2,128,512]{2,1,0:T(8,128)(2,1)S(1)} %collective-permute-done.4.refs_6_.refs_7_), channel_id=1, source_target_pairs={{0,1},{1,0},{2,3},{3,2},{4,5},{5,4},{6,7},{7,6},{8,9},{9,8},{10,11... | collective-permute-start | bytes 786440 | tf_op jit(solution)/shard_map/ppermute | solution.py:128
  29.2 14.8 %copy-start.3 = (bf16[2,128,512]{2,1,0:T(8,128)(2,1)}, bf16[2,128,512]{2,1,0:T(8,128)(2,1)S(1)}, u32[]{:S(2)}) copy-start(bf16[2,128,512]{2,1,0:T(8,128)(2,1)S(1)} %collective-permute-done.refs_1_.refs_2_) | copy-start | bytes 786436
  29.2 16.3 %collective-permute-start.2 = (bf16[2,128,512]{2,1,0:T(8,128)(2,1)S(1)}, bf16[2,128,512]{2,1,0:T(8,128)(2,1)}, u32[]{:S(2)}, u32[]{:S(2)}) collective-permute-start(bf16[2,128,512]{2,1,0:T(8,128)(2,1)S(1)} %collective-permute-done.refs_1_.refs_2_), channel_id=1, source_target_pairs={{0,2},{1,3},{2,0},{3,1},{4,6},{5,7},{6,4},{7,5},{8,10},{9,11},{10,... | collective-permute-start | bytes 786440 | tf_op jit(solution)/shard_map/ppermute | solution.py:128
  39.0 25.9 %all-to-all-start = ((bf16[8,384,128]{2,1,0:T(8,128)(2,1)}), bf16[8,384,128]{2,1,0:T(8,128)(2,1)}, u32[]{:S(2)}, u32[]{:S(2)}) async-start(bf16[8,384,128]{2,1,0:T(8,128)(2,1)} %get-tuple-element.7), calls=%async_computation | async-start | bytes 1572864 | tf_op jit(solution)/shard_map/all_to_all | solution.py:390
  44.0 0.7 copy-start.4
  44.0 0.8 copy-start.5
  44.8 0.7 copy-start.6

commit v3 on v2

--- a/solution.py
+++ b/solution.py
@@ -17,7 +17,8 @@
 
 
 def lookup_kernel(cuts, ids, counts, table_t, *refs):
-    outs, refs = refs[: len(cuts) - 1], refs[len(cuts) - 1 :]
+    chunks = len(cuts) - 1
+    outs, packed, put_sems, refs = refs[:chunks], refs[-chunks - 1 : -1], refs[-1], refs[chunks : -chunks - 1]
     table, rows_major, found, picked, id_vector, local_ids, held, sems = refs
     columns, vocab = table_t.shape
     groups = counts.shape[0]
@@ -75,18 +76,24 @@
 
     lax.fori_loop(0, groups, sender, (jnp.int32(0),) * groups)
 
-    def pack(group, carry):
-        for low, out in zip(cuts, outs):
-            part = out.shape[1]
-            lane = lax.broadcasted_iota(jnp.int32, (part, LANES), 1) // columns
+    puts = []
+    for chunk, (low, out) in enumerate(zip(cuts, outs)):
+        part = out.shape[1]
+        lane = lax.broadcasted_iota(jnp.int32, (part, LANES), 1) // columns
+        for group in range(groups):
             value = picked[group, pl.ds(low, part), :]
             for piece in range(1, packing):
                 more = picked[group, pl.ds(low + piece * part, part), :]
                 value = jnp.where(lane == piece, more, value)
-            out[group] = value.astype(jnp.bfloat16)
-        return carry
-
-    lax.fori_loop(0, groups, pack, 0)
+            packed[chunk][group] = value.astype(jnp.bfloat16)
+            puts.append(
+                pltpu.make_async_copy(
+                    packed[chunk].at[group], out.at[group], put_sems.at[len(puts)]
+                )
+            )
+            puts[-1].start()
+    for copy in puts:
+        copy.wait()
 
 
 def lookup(ids, counts, table_t, cuts):
@@ -101,7 +108,7 @@
             for low, high in zip(cuts, cuts[1:])
         ),
         in_specs=[ANY, ANY, ANY],
-        out_specs=(VMEM,) * (len(cuts) - 1),
+        out_specs=(ANY,) * (len(cuts) - 1),
         scratch_shapes=[
             pltpu.VMEM((columns, vocab), jnp.bfloat16),
             pltpu.VMEM((vocab, LANES), jnp.float32),
@@ -111,7 +118,12 @@
             pltpu.SMEM(ids.shape, jnp.int32),
             pltpu.SMEM(counts.shape, jnp.int32),
             pltpu.SemaphoreType.DMA((11,)),
-        ],
+        ]
+        + [
+            pltpu.VMEM((groups, (high - low) // packing, LANES), jnp.bfloat16)
+            for low, high in zip(cuts, cuts[1:])
+        ]
+        + [pltpu.SemaphoreType.DMA((groups * (len(cuts) - 1),))],
         compiler_params=pltpu.CompilerParams(vmem_limit_bytes=64 * MIB - MIB // 4),
         name="lookup",
     )(ids, counts, table_t)
@@ -163,11 +175,12 @@
     return [values[:, at : at + LANES] for at in range(0, values.shape[1], LANES)]
 
 
-def rank_kernel(low, capacity, done, shards, counts, lengths, pieces, *refs):
+def rank_kernel(low, capacity, done, shards, counts_in_hbm, lengths_in_hbm, pieces, *refs):
     before, refs = refs[:done], refs[done:]
     history, refs = refs[: 2 * shards], refs[2 * shards :]
     weights, out, refs = refs[:4], refs[4], refs[5:]
     ranked, refs = (refs[0], refs[1:]) if done else (None, refs)
+    counts, lengths, refs = refs[0], refs[1], refs[2:]
     got, keys, values, w_in, w_out, w_proj, w_back, sems, refs = *refs[:8], refs[8:]
     pieces_in_hbm, pieces = pieces, got
     groups, part, _ = pieces.shape
@@ -177,15 +190,47 @@
     tile = part * packing
     table_index = lax.axis_index("table")
     shard = lax.axis_index("seq")
+    last_sem = sems.shape[0] - 1
+    get_numbers = [
+        pltpu.make_async_copy(counts_in_hbm, counts, sems.at[last_sem]),
+        pltpu.make_async_copy(lengths_in_hbm, lengths, sems.at[last_sem - 1]),
+    ]
+    for copy in get_numbers:
+        copy.start()
+    get_pieces = pltpu.make_async_copy(pieces_in_hbm, pieces, sems.at[last_sem - 2])
+    get_before = []
+    for k, piece in enumerate(before):
+        get_before.append(pltpu.make_async_copy(piece, refs[k], sems.at[last_sem - 3 - k]))
+        get_before[-1].start()
+
+    chunk = width
+    head, tail = pl.ds(0, chunk), pl.ds(chunk, w_in.shape[1] - chunk)
+    views = [
+        (weights[0].at[:, head], w_in.at[:, head]),
+        (weights[1].at[head], w_out.at[head]),
+        (weights[0].at[:, tail], w_in.at[:, tail]),
+        (weights[1].at[tail], w_out.at[tail]),
+        (weights[2], w_proj),
+        (weights[3], w_back),
+    ]
+    piece_rows = keys.shape[1] // shards
+    for k in range(2 * shards):
+        place = pl.multiple_of((shard ^ (k % shards)) * piece_rows, piece_rows)
+        target = (keys, values)[k // shards]
+        views.append((history[k], target.at[:, pl.ds(place, piece_rows), :]))
+    copies = [
+        pltpu.make_async_copy(source, target, sems.at[k])
+        for k, (source, target) in enumerate(views)
+    ]
+    copies[0].start()
+    get_pieces.start()
+    for copy in copies[1:4]:
+        copy.start()
+    for copy in get_numbers:
+        copy.wait()
     filled = lax.fori_loop(
         0, groups, lambda t, n: n + counts[t, shard, table_index], jnp.int32(0)
     )
-
-    get_pieces = pltpu.make_async_copy(pieces_in_hbm, pieces, sems.at[sems.shape[0] - 1])
-    get_before = []
-    for k, piece in enumerate(before):
-        get_before.append(pltpu.make_async_copy(piece, refs[k], sems.at[sems.shape[0] - 2 - k]))
-        get_before[-1].start()
 
     def keep(states):
         if done:
@@ -234,29 +279,6 @@
 
     @pl.when(low < filled)
     def _():
-        chunk = width
-        head, tail = pl.ds(0, chunk), pl.ds(chunk, w_in.shape[1] - chunk)
-        views = [
-            (weights[0].at[:, head], w_in.at[:, head]),
-            (weights[1].at[head], w_out.at[head]),
-            (weights[0].at[:, tail], w_in.at[:, tail]),
-            (weights[1].at[tail], w_out.at[tail]),
-            (weights[2], w_proj),
-            (weights[3], w_back),
-        ]
-        piece_rows = keys.shape[1] // shards
-        for k in range(2 * shards):
-            place = pl.multiple_of((shard ^ (k % shards)) * piece_rows, piece_rows)
-            target = (keys, values)[k // shards]
-            views.append((history[k], target.at[:, pl.ds(place, piece_rows), :]))
-        copies = [
-            pltpu.make_async_copy(source, target, sems.at[k])
-            for k, (source, target) in enumerate(views)
-        ]
-        copies[0].start()
-        get_pieces.start()
-        for copy in copies[1:4]:
-            copy.start()
         if done:
             fill_before()
             fill_slots(True)
@@ -336,13 +358,16 @@
             states = (states.astype(jnp.float32) + dot(mixed, w_back[layer])).astype(jnp.bfloat16)
         keep(states)
 
-    if done:
-
-        @pl.when(low >= filled)
-        def _():
+    @pl.when(low >= filled)
+    def _():
+        for copy in copies[:4]:
+            copy.wait()
+        get_pieces.wait()
+        if done:
             fill_before()
             fill_slots(True)
 
+    if done:
         fill_slots(False)
         for sender in range(groups):
             put(sender).wait()
@@ -356,10 +381,11 @@
     done = len(before)
     layers, piece_rows, _ = history[0].shape
     shards = len(history) // 2
-    scratch = [pltpu.VMEM(pieces.shape, pieces.dtype)]
+    numbers = [pltpu.SMEM(counts.shape, jnp.int32), pltpu.SMEM(lengths.shape, jnp.int32)]
+    scratch = numbers + [pltpu.VMEM(pieces.shape, pieces.dtype)]
     scratch += [pltpu.VMEM((layers, shards * piece_rows, width), jnp.bfloat16)] * 2
     scratch += [pltpu.VMEM(weight.shape, weight.dtype) for weight in weights]
-    scratch += [pltpu.SemaphoreType.DMA((len(weights) + 3 + len(history) + done,))]
+    scratch += [pltpu.SemaphoreType.DMA((len(weights) + 5 + len(history) + done,))]
     if done:
         scratch = [pltpu.VMEM((width // LANES, total + capacity, LANES), jnp.float32)] + scratch
         scratch += [pltpu.VMEM(piece.shape, piece.dtype) for piece in before]
@@ -367,7 +393,7 @@
     return pl.pallas_call(
         functools.partial(rank_kernel, low, capacity, done, shards),
         out_shape=jax.ShapeDtypeStruct((total if done else tile, width), jnp.bfloat16),
-        in_specs=[SMEM, SMEM] + [ANY] * (1 + done + len(history) + len(weights)),
+        in_specs=[ANY] * (3 + done + len(history) + len(weights)),
         out_specs=ANY if done else VMEM,
         scratch_shapes=scratch,
         compiler_params=pltpu.CompilerParams(vmem_limit_bytes=64 * MIB - MIB // 4),
@@ -383,7 +409,8 @@
     row_count = item_ids.shape[0] // groups
     capacity = 3 * row_count // (2 * groups)
     total = groups * capacity
-    cuts = (0, total // 2, total)
+    packing = LANES // item_table.shape[1]
+    cuts = (0, total * 25 // 48 // (16 * packing) * (16 * packing), total)
     table_t = item_table.T
     found = lookup(item_ids, group_counts, table_t, cuts)
     pieces = [

time: 85.5 us -> 83.3 us (0.974)
  Pallas kernels: 51.7 us -> 48.9 us
    pallas_call x2, Pallas kernels: 39.3 us -> 36.7 us  [rank(): pl.pallas_call(functools.partial(rank_kernel, low, capacity, done, shards...]
where the time goes in v3:
time: 83.3 us; the launch traced here: 82.9 us
  Pallas kernels  48.9 us (59%)
  starting transfers between devices  16.9 us (20%)
  waiting for transfers between devices  14.2 us (17%)
  local copies, waits for them, and re-layouts  2.52 us (3%)
    pallas_call x2, Pallas kernels, rank(): pl.pallas_call(functools.partial(rank_kernel, low, capacity, done, shards...  36.7 us
    pallas_call x1, Pallas kernels, lookup(): pl.pallas_call(functools.partial(lookup_kernel, cuts), out_shape=tuple((j...  12.2 us
    all_to_all x2, starting transfers between devices, local(): lax.all_to_all(chunk, 'table', split_axis=0, concat_axis=0, tiled=True)  11.3 us
    all_to_all x2, waiting for transfers between devices, local(): lax.all_to_all(chunk, 'table', split_axis=0, concat_axis=0, tiled=True)  9.27 us
    ppermute x6, starting transfers between devices, gather_history(): lax.ppermute(v, 'seq', route)  5.59 us
    ppermute x6, waiting for transfers between devices, gather_history(): lax.ppermute(v, 'seq', route)  4.98 us
  transfers between devices with their start and end apart: 8, of which 2 were waited for; matrix products, arithmetic and copies ran while one was open for 1% of the time, Pallas kernels for 23%

profile of v3, /device:TPU:1, one launch (start us, length us, event | category | flops | bytes accessed | tf_op | source)
XLA Modules:
  0.0 82.9 jit_solution(17967368693575856279)
XLA Ops:
  0.0 12.2 %lookup.1 = (bf16[8,400,128]{2,1,0:T(8,128)(2,1)}, bf16[8,368,128]{2,1,0:T(8,128)(2,1)}) custom-call(s32[8192]{0:T(1024)} %ids.1, s32[8,4,8]{2,1,0:T(4,128)} %counts_in_hbm.3, bf16[64,32768]{1,0:T(8,128)(2,1)} %bitcast.9), custom_call_target="tpu_custom_call" | custom-call | tf_op jit(solution)/shard_map/lookup/pallas_call | solution.py:104
  12.2 6.4 %all-to-all-start.1 = ((bf16[8,400,128]{2,1,0:T(8,128)(2,1)}), bf16[8,400,128]{2,1,0:T(8,128)(2,1)}, u32[]{:S(2)}, u32[]{:S(2)}) async-start(bf16[8,400,128]{2,1,0:T(8,128)(2,1)} %get-tuple-element.8), calls=%async_computation.1 | async-start | bytes 1638400 | tf_op jit(solution)/shard_map/all_to_all | solution.py:417
  18.6 1.1 %slice_bitcast_fusion = (bf16[2,128,512]{2,1,0:T(8,128)(2,1)S(1)}, bf16[2,128,512]{2,1,0:T(8,128)(2,1)S(1)}) fusion(bf16[1,2,2,128,512]{4,3,2,1,0:T(8,128)(2,1)} %param.13), kind=kLoop, calls=%fused_computation | loop fusion | bytes 1048576 | tf_op jit(solution)/shard_map/squeeze | solution.py:137
  19.7 0.0 copy-start
  19.7 0.0 copy-start.1
  19.7 1.3 %collective-permute-start.4 = (bf16[2,128,512]{2,1,0:T(8,128)(2,1)S(1)}, bf16[2,128,512]{2,1,0:T(8,128)(2,1)S(1)}, u32[]{:S(2)}, u32[]{:S(2)}) collective-permute-start(bf16[2,128,512]{2,1,0:T(8,128)(2,1)S(1)} %get-tuple-element.9.refs_4_.refs_5_), channel_id=1, source_target_pairs={{0,2},{1,3},{2,0},{3,1},{4,6},{5,7},{6,4},{7,5},{8,10},{9,11},{10,... | collective-permute-start | bytes 786440 | tf_op jit(solution)/shard_map/ppermute | solution.py:140
  21.0 1.2 %collective-permute-start = (bf16[2,128,512]{2,1,0:T(8,128)(2,1)S(1)}, bf16[2,128,512]{2,1,0:T(8,128)(2,1)S(1)}, u32[]{:S(2)}, u32[]{:S(2)}) collective-permute-start(bf16[2,128,512]{2,1,0:T(8,128)(2,1)S(1)} %get-tuple-element.10.refs_0_.refs_1_), channel_id=1, source_target_pairs={{0,1},{1,0},{2,3},{3,2},{4,5},{5,4},{6,7},{7,6},{8,9},{9,8},{10,11... | collective-permute-start | bytes 786440 | tf_op jit(solution)/shard_map/ppermute | solution.py:140
  22.2 0.0 copy-done
  22.2 0.3 collective-permute-start.3
  22.5 0.4 collective-permute-start.1
  22.8 5.0 %collective-permute-done.4.refs_6_.refs_7_ = bf16[2,128,512]{2,1,0:T(8,128)(2,1)S(1)} collective-permute-done((bf16[2,128,512]{2,1,0:T(8,128)(2,1)S(1)}, bf16[2,128,512]{2,1,0:T(8,128)(2,1)S(1)}, u32[]{:S(2)}, u32[]{:S(2)}) %collective-permute-start.4) | collective-permute-done | bytes 262176 | tf_op jit(solution)/shard_map/ppermute | solution.py:140
  27.8 0.0 copy-start.2
  27.8 1.2 %collective-permute-start.5 = (bf16[2,128,512]{2,1,0:T(8,128)(2,1)S(1)}, bf16[2,128,512]{2,1,0:T(8,128)(2,1)S(1)}, u32[]{:S(2)}, u32[]{:S(2)}) collective-permute-start(bf16[2,128,512]{2,1,0:T(8,128)(2,1)S(1)} %collective-permute-done.4.refs_6_.refs_7_), channel_id=1, source_target_pairs={{0,1},{1,0},{2,3},{3,2},{4,5},{5,4},{6,7},{7,6},{8,9},{9,8},{10,11... | collective-permute-start | bytes 786440 | tf_op jit(solution)/shard_map/ppermute | solution.py:140
  29.0 0.0 collective-permute-done.refs_1_.refs_2_
  29.0 0.0 copy-start.3
  29.0 1.2 %collective-permute-start.2 = (bf16[2,128,512]{2,1,0:T(8,128)(2,1)S(1)}, bf16[2,128,512]{2,1,0:T(8,128)(2,1)}, u32[]{:S(2)}, u32[]{:S(2)}) collective-permute-start(bf16[2,128,512]{2,1,0:T(8,128)(2,1)S(1)} %collective-permute-done.refs_1_.refs_2_), channel_id=1, source_target_pairs={{0,2},{1,3},{2,0},{3,1},{4,6},{5,7},{6,4},{7,5},{8,10},{9,11},{10,... | collective-permute-start | bytes 786440 | tf_op jit(solution)/shard_map/ppermute | solution.py:140
  30.2 9.3 %all-to-all-done.1.pieces = bf16[8,400,128]{2,1,0:T(8,128)(2,1)} async-done(((bf16[8,400,128]{2,1,0:T(8,128)(2,1)}), bf16[8,400,128]{2,1,0:T(8,128)(2,1)}, u32[]{:S(2)}, u32[]{:S(2)}) %all-to-all-start.1) | async-done | bytes 819232 | tf_op jit(solution)/shard_map/all_to_all | solution.py:417
  39.5 5.0 %all-to-all-start = ((bf16[8,368,128]{2,1,0:T(8,128)(2,1)}), bf16[8,368,128]{2,1,0:T(8,128)(2,1)}, u32[]{:S(2)}, u32[]{:S(2)}) async-start(bf16[8,368,128]{2,1,0:T(8,128)(2,1)} %get-tuple-element.7), calls=%async_computation | async-start | bytes 1507328 | tf_op jit(solution)/shard_map/all_to_all | solution.py:417
  44.5 0.0 collective-permute-done.3.refs_5_.refs_6_
  44.5 0.0 copy-done.1
  44.5 0.0 copy-start.4
  44.5 0.0 collective-permute-done.1.refs_2_.refs_3_
  44.5 0.0 copy-done.2
  44.5 0.0 copy-start.5
  44.5 0.0 collective-permute-done.5.refs_7_.refs_8_
  44.5 0.0 copy-done.3
  44.5 0.6 copy-done.4
  45.2 0.1 copy-done.5
  45.3 0.0 copy-start.6
  45.3 0.7 copy-done.6
  46.0 0.0 collective-permute-done.2.refs_3_.refs_4_
  46.0 19.0 %rank.2.refs_0_ = bf16[800,512]{1,0:T(8,128)(2,1)} custom-call(s32[8,4,8]{2,1,0:T(4,128)} %counts_in_hbm.3, s32[8]{0:T(128)} %lengths_in_hbm.3, bf16[8,400,128]{2,1,0:T(8,128)(2,1)} %all-to-all-done.1.pieces, bf16[2,128,512]{2,1,0:T(8,128)(2,1)} %copy-done.1, bf16[2,128,512]{2,1,0:T(8,128)(2,1)} %copy-done.3, bf16[2,128,512]{2,1,0:T(8,128)(2,1)} %copy-done.5, ...), custom_call_target="tpu_custom_call" | custom-call | flops 20000000000 | bytes 20000000 | tf_op jit(solution)/shard_map/rank/pallas_call | solution.py:393
  64.9 0.0 all-to-all-done.pieces
  65.0 17.7 %rank.3 = bf16[1536,512]{1,0:T(8,128)(2,1)} custom-call(s32[8,4,8]{2,1,0:T(4,128)} %counts_in_hbm.3, s32[8]{0:T(128)} %lengths_in_hbm.3, bf16[8,368,128]{2,1,0:T(8,128)(2,1)} %all-to-all-done.pieces, bf16[800,512]{1,0:T(8,128)(2,1)} %rank.2.refs_0_, bf16[2,128,512]{2,1,0:T(8,128)(2,1)} %copy-done.1, bf16[2,128,512]{2,1,0:T(8,128)(2,1)} %copy-done.3, ...), custom_call_target="tpu_custom_call" | custom-call | flops 20000000000 | bytes 20000000 | tf_op jit(solution)/shard_map/rank/pallas_call | solution.py:393
Async XLA Ops:
  12.2 27.3 %all-to-all-start.1 = ((bf16[8,400,128]{2,1,0:T(8,128)(2,1)}), bf16[8,400,128]{2,1,0:T(8,128)(2,1)}, u32[]{:S(2)}, u32[]{:S(2)}) async-start(bf16[8,400,128]{2,1,0:T(8,128)(2,1)} %get-tuple-element.8), calls=%async_computation.1 | async-start | bytes 1638400 | tf_op jit(solution)/shard_map/all_to_all | solution.py:417
  19.7 2.5 %copy-start = (bf16[2,128,512]{2,1,0:T(8,128)(2,1)}, bf16[2,128,512]{2,1,0:T(8,128)(2,1)S(1)}, u32[]{:S(2)}) copy-start(bf16[2,128,512]{2,1,0:T(8,128)(2,1)S(1)} %get-tuple-element.9.refs_4_.refs_5_) | copy-start | bytes 786436
  19.7 24.8 %copy-start.1 = (bf16[2,128,512]{2,1,0:T(8,128)(2,1)}, bf16[2,128,512]{2,1,0:T(8,128)(2,1)S(1)}, u32[]{:S(2)}) copy-start(bf16[2,128,512]{2,1,0:T(8,128)(2,1)S(1)} %get-tuple-element.10.refs_0_.refs_1_) | copy-start | bytes 786436
  19.7 8.1 %collective-permute-start.4 = (bf16[2,128,512]{2,1,0:T(8,128)(2,1)S(1)}, bf16[2,128,512]{2,1,0:T(8,128)(2,1)S(1)}, u32[]{:S(2)}, u32[]{:S(2)}) collective-permute-start(bf16[2,128,512]{2,1,0:T(8,128)(2,1)S(1)} %get-tuple-element.9.refs_4_.refs_5_), channel_id=1, source_target_pairs={{0,2},{1,3},{2,0},{3,1},{4,6},{5,7},{6,4},{7,5},{8,10},{9,11},{10,... | collective-permute-start | bytes 786440 | tf_op jit(solution)/shard_map/ppermute | solution.py:140
  21.0 8.0 %collective-permute-start = (bf16[2,128,512]{2,1,0:T(8,128)(2,1)S(1)}, bf16[2,128,512]{2,1,0:T(8,128)(2,1)S(1)}, u32[]{:S(2)}, u32[]{:S(2)}) collective-permute-start(bf16[2,128,512]{2,1,0:T(8,128)(2,1)S(1)} %get-tuple-element.10.refs_0_.refs_1_), channel_id=1, source_target_pairs={{0,1},{1,0},{2,3},{3,2},{4,5},{5,4},{6,7},{7,6},{8,9},{9,8},{10,11... | collective-permute-start | bytes 786440 | tf_op jit(solution)/shard_map/ppermute | solution.py:140
  22.2 22.3 %collective-permute-start.3 = (bf16[2,128,512]{2,1,0:T(8,128)(2,1)S(1)}, bf16[2,128,512]{2,1,0:T(8,128)(2,1)S(1)}, u32[]{:S(2)}, u32[]{:S(2)}) collective-permute-start(bf16[2,128,512]{2,1,0:T(8,128)(2,1)S(1)} %get-tuple-element.9.refs_4_.refs_5_), channel_id=1, source_target_pairs={{0,1},{1,0},{2,3},{3,2},{4,5},{5,4},{6,7},{7,6},{8,9},{9,8},{10,11... | collective-permute-start | bytes 786440 | tf_op jit(solution)/shard_map/ppermute | solution.py:140
  22.5 22.0 %collective-permute-start.1 = (bf16[2,128,512]{2,1,0:T(8,128)(2,1)S(1)}, bf16[2,128,512]{2,1,0:T(8,128)(2,1)S(1)}, u32[]{:S(2)}, u32[]{:S(2)}) collective-permute-start(bf16[2,128,512]{2,1,0:T(8,128)(2,1)S(1)} %get-tuple-element.10.refs_0_.refs_1_), channel_id=1, source_target_pairs={{0,2},{1,3},{2,0},{3,1},{4,6},{5,7},{6,4},{7,5},{8,10},{9,11},{10,... | collective-permute-start | bytes 786440 | tf_op jit(solution)/shard_map/ppermute | solution.py:140
  27.8 16.7 %copy-start.2 = (bf16[2,128,512]{2,1,0:T(8,128)(2,1)}, bf16[2,128,512]{2,1,0:T(8,128)(2,1)S(1)}, u32[]{:S(2)}) copy-start(bf16[2,128,512]{2,1,0:T(8,128)(2,1)S(1)} %collective-permute-done.4.refs_6_.refs_7_) | copy-start | bytes 786436
  27.8 16.7 %collective-permute-start.5 = (bf16[2,128,512]{2,1,0:T(8,128)(2,1)S(1)}, bf16[2,128,512]{2,1,0:T(8,128)(2,1)S(1)}, u32[]{:S(2)}, u32[]{:S(2)}) collective-permute-start(bf16[2,128,512]{2,1,0:T(8,128)(2,1)S(1)} %collective-permute-done.4.refs_6_.refs_7_), channel_id=1, source_target_pairs={{0,1},{1,0},{2,3},{3,2},{4,5},{5,4},{6,7},{7,6},{8,9},{9,8},{10,11... | collective-permute-start | bytes 786440 | tf_op jit(solution)/shard_map/ppermute | solution.py:140
  29.0 15.5 %copy-start.3 = (bf16[2,128,512]{2,1,0:T(8,128)(2,1)}, bf16[2,128,512]{2,1,0:T(8,128)(2,1)S(1)}, u32[]{:S(2)}) copy-start(bf16[2,128,512]{2,1,0:T(8,128)(2,1)S(1)} %collective-permute-done.refs_1_.refs_2_) | copy-start | bytes 786436
  29.0 17.0 %collective-permute-start.2 = (bf16[2,128,512]{2,1,0:T(8,128)(2,1)S(1)}, bf16[2,128,512]{2,1,0:T(8,128)(2,1)}, u32[]{:S(2)}, u32[]{:S(2)}) collective-permute-start(bf16[2,128,512]{2,1,0:T(8,128)(2,1)S(1)} %collective-permute-done.refs_1_.refs_2_), channel_id=1, source_target_pairs={{0,2},{1,3},{2,0},{3,1},{4,6},{5,7},{6,4},{7,5},{8,10},{9,11},{10,... | collective-permute-start | bytes 786440 | tf_op jit(solution)/shard_map/ppermute | solution.py:140
  39.5 25.4 %all-to-all-start = ((bf16[8,368,128]{2,1,0:T(8,128)(2,1)}), bf16[8,368,128]{2,1,0:T(8,128)(2,1)}, u32[]{:S(2)}, u32[]{:S(2)}) async-start(bf16[8,368,128]{2,1,0:T(8,128)(2,1)} %get-tuple-element.7), calls=%async_computation | async-start | bytes 1507328 | tf_op jit(solution)/shard_map/all_to_all | solution.py:417
  44.5 0.7 copy-start.4
  44.5 0.8 copy-start.5
  45.3 0.7 copy-start.6

commit v4 on v3

--- a/solution.py
+++ b/solution.py
@@ -233,13 +233,10 @@
     )
 
     def keep(states):
-        if done:
-            for block in range(width // LANES):
-                ranked[block, pl.ds(low, tile), :] = states[
-                    :, block * LANES : (block + 1) * LANES
-                ].astype(jnp.float32)
-        else:
-            out[...] = states
+        for block in range(width // LANES):
+            ranked[block, pl.ds(low, tile), :] = states[
+                :, block * LANES : (block + 1) * LANES
+            ].astype(jnp.float32)
 
     if done:
         slots, put_sems = refs[done], refs[done + 1]
@@ -355,8 +352,25 @@
                 for block, open_ in zip(normalized(attended), in_blocks(gate))
             ]
             mixed = jnp.concatenate(mixed, axis=1)
+            if layer + 1 == w_proj.shape[0] and not done:
+                continue
             states = (states.astype(jnp.float32) + dot(mixed, w_back[layer])).astype(jnp.bfloat16)
-        keep(states)
+        if done:
+            keep(states)
+        else:
+            staged, put_sems = refs
+            puts = []
+            middle = tile // 32 * 16
+            for k, (at, end) in enumerate(((0, middle), (middle, tile))):
+                more = dot(mixed[at:end], w_back[w_proj.shape[0] - 1])
+                rows = pl.ds(at, end - at)
+                staged[rows, :] = (states[at:end].astype(jnp.float32) + more).astype(jnp.bfloat16)
+                puts.append(
+                    pltpu.make_async_copy(staged.at[rows], out.at[rows], put_sems.at[k])
+                )
+                puts[-1].start()
+            for copy in puts:
+                copy.wait()
 
     @pl.when(low >= filled)
     def _():
@@ -390,11 +404,13 @@
         scratch = [pltpu.VMEM((width // LANES, total + capacity, LANES), jnp.float32)] + scratch
         scratch += [pltpu.VMEM(piece.shape, piece.dtype) for piece in before]
         scratch += [pltpu.VMEM((total, width), jnp.bfloat16), pltpu.SemaphoreType.DMA((groups,))]
+    else:
+        scratch += [pltpu.VMEM((tile, width), jnp.bfloat16), pltpu.SemaphoreType.DMA((2,))]
     return pl.pallas_call(
         functools.partial(rank_kernel, low, capacity, done, shards),
         out_shape=jax.ShapeDtypeStruct((total if done else tile, width), jnp.bfloat16),
         in_specs=[ANY] * (3 + done + len(history) + len(weights)),
-        out_specs=ANY if done else VMEM,
+        out_specs=ANY,
         scratch_shapes=scratch,
         compiler_params=pltpu.CompilerParams(vmem_limit_bytes=64 * MIB - MIB // 4),
         cost_estimate=pl.CostEstimate(

time: 83.3 us -> 83.1 us (level)
  no operation moved by 1% of the time
where the time goes in v4:
time: 83.1 us; the launch traced here: 82.5 us
  Pallas kernels  48.5 us (58%)
  starting transfers between devices  16.9 us (20%)
  waiting for transfers between devices  14.2 us (17%)
  local copies, waits for them, and re-layouts  2.52 us (3%)
    pallas_call x2, Pallas kernels, rank(): pl.pallas_call(functools.partial(rank_kernel, low, capacity, done, shards...  36.3 us
    pallas_call x1, Pallas kernels, lookup(): pl.pallas_call(functools.partial(lookup_kernel, cuts), out_shape=tuple((j...  12.2 us
    all_to_all x2, starting transfers between devices, local(): lax.all_to_all(chunk, 'table', split_axis=0, concat_axis=0, tiled=True)  11.3 us
    all_to_all x2, waiting for transfers between devices, local(): lax.all_to_all(chunk, 'table', split_axis=0, concat_axis=0, tiled=True)  9.26 us
    ppermute x6, starting transfers between devices, gather_history(): lax.ppermute(v, 'seq', route)  5.59 us
    ppermute x6, waiting for transfers between devices, gather_history(): lax.ppermute(v, 'seq', route)  4.98 us
  transfers between devices with their start and end apart: 8, of which 2 were waited for; matrix products, arithmetic and copies ran while one was open for 1% of the time, Pallas kernels for 23%

profile of v4, /device:TPU:1, one launch (start us, length us, event | category | flops | bytes accessed | tf_op | source)
XLA Modules:
  0.0 82.5 jit_solution(2778775265453518057)
XLA Ops:
  0.0 12.2 %lookup.1 = (bf16[8,400,128]{2,1,0:T(8,128)(2,1)}, bf16[8,368,128]{2,1,0:T(8,128)(2,1)}) custom-call(s32[8192]{0:T(1024)} %ids.1, s32[8,4,8]{2,1,0:T(4,128)} %counts_in_hbm.3, bf16[64,32768]{1,0:T(8,128)(2,1)} %bitcast.9), custom_call_target="tpu_custom_call" | custom-call | tf_op jit(solution)/shard_map/lookup/pallas_call | solution.py:104
  12.2 6.4 %all-to-all-start.1 = ((bf16[8,400,128]{2,1,0:T(8,128)(2,1)}), bf16[8,400,128]{2,1,0:T(8,128)(2,1)}, u32[]{:S(2)}, u32[]{:S(2)}) async-start(bf16[8,400,128]{2,1,0:T(8,128)(2,1)} %get-tuple-element.8), calls=%async_computation.1 | async-start | bytes 1638400 | tf_op jit(solution)/shard_map/all_to_all | solution.py:433
  18.6 1.1 %slice_bitcast_fusion = (bf16[2,128,512]{2,1,0:T(8,128)(2,1)S(1)}, bf16[2,128,512]{2,1,0:T(8,128)(2,1)S(1)}) fusion(bf16[1,2,2,128,512]{4,3,2,1,0:T(8,128)(2,1)} %param.13), kind=kLoop, calls=%fused_computation | loop fusion | bytes 1048576 | tf_op jit(solution)/shard_map/squeeze | solution.py:137
  19.7 0.0 copy-start
  19.7 0.0 copy-start.1
  19.7 1.3 %collective-permute-start.4 = (bf16[2,128,512]{2,1,0:T(8,128)(2,1)S(1)}, bf16[2,128,512]{2,1,0:T(8,128)(2,1)S(1)}, u32[]{:S(2)}, u32[]{:S(2)}) collective-permute-start(bf16[2,128,512]{2,1,0:T(8,128)(2,1)S(1)} %get-tuple-element.9.refs_4_.refs_5_), channel_id=1, source_target_pairs={{0,2},{1,3},{2,0},{3,1},{4,6},{5,7},{6,4},{7,5},{8,10},{9,11},{10,... | collective-permute-start | bytes 786440 | tf_op jit(solution)/shard_map/ppermute | solution.py:140
  21.0 1.2 %collective-permute-start = (bf16[2,128,512]{2,1,0:T(8,128)(2,1)S(1)}, bf16[2,128,512]{2,1,0:T(8,128)(2,1)S(1)}, u32[]{:S(2)}, u32[]{:S(2)}) collective-permute-start(bf16[2,128,512]{2,1,0:T(8,128)(2,1)S(1)} %get-tuple-element.10.refs_0_.refs_1_), channel_id=1, source_target_pairs={{0,1},{1,0},{2,3},{3,2},{4,5},{5,4},{6,7},{7,6},{8,9},{9,8},{10,11... | collective-permute-start | bytes 786440 | tf_op jit(solution)/shard_map/ppermute | solution.py:140
  22.2 0.0 copy-done
  22.2 0.3 collective-permute-start.3
  22.5 0.4 collective-permute-start.1
  22.8 5.0 %collective-permute-done.4.refs_6_.refs_7_ = bf16[2,128,512]{2,1,0:T(8,128)(2,1)S(1)} collective-permute-done((bf16[2,128,512]{2,1,0:T(8,128)(2,1)S(1)}, bf16[2,128,512]{2,1,0:T(8,128)(2,1)S(1)}, u32[]{:S(2)}, u32[]{:S(2)}) %collective-permute-start.4) | collective-permute-done | bytes 262176 | tf_op jit(solution)/shard_map/ppermute | solution.py:140
  27.8 0.0 copy-start.2
  27.8 1.2 %collective-permute-start.5 = (bf16[2,128,512]{2,1,0:T(8,128)(2,1)S(1)}, bf16[2,128,512]{2,1,0:T(8,128)(2,1)S(1)}, u32[]{:S(2)}, u32[]{:S(2)}) collective-permute-start(bf16[2,128,512]{2,1,0:T(8,128)(2,1)S(1)} %collective-permute-done.4.refs_6_.refs_7_), channel_id=1, source_target_pairs={{0,1},{1,0},{2,3},{3,2},{4,5},{5,4},{6,7},{7,6},{8,9},{9,8},{10,11... | collective-permute-start | bytes 786440 | tf_op jit(solution)/shard_map/ppermute | solution.py:140
  29.0 0.0 collective-permute-done.refs_1_.refs_2_
  29.0 0.0 copy-start.3
  29.0 1.2 %collective-permute-start.2 = (bf16[2,128,512]{2,1,0:T(8,128)(2,1)S(1)}, bf16[2,128,512]{2,1,0:T(8,128)(2,1)}, u32[]{:S(2)}, u32[]{:S(2)}) collective-permute-start(bf16[2,128,512]{2,1,0:T(8,128)(2,1)S(1)} %collective-permute-done.refs_1_.refs_2_), channel_id=1, source_target_pairs={{0,2},{1,3},{2,0},{3,1},{4,6},{5,7},{6,4},{7,5},{8,10},{9,11},{10,... | collective-permute-start | bytes 786440 | tf_op jit(solution)/shard_map/ppermute | solution.py:140
  30.3 9.3 %all-to-all-done.1.pieces = bf16[8,400,128]{2,1,0:T(8,128)(2,1)} async-done(((bf16[8,400,128]{2,1,0:T(8,128)(2,1)}), bf16[8,400,128]{2,1,0:T(8,128)(2,1)}, u32[]{:S(2)}, u32[]{:S(2)}) %all-to-all-start.1) | async-done | bytes 819232 | tf_op jit(solution)/shard_map/all_to_all | solution.py:433
  39.5 5.0 %all-to-all-start = ((bf16[8,368,128]{2,1,0:T(8,128)(2,1)}), bf16[8,368,128]{2,1,0:T(8,128)(2,1)}, u32[]{:S(2)}, u32[]{:S(2)}) async-start(bf16[8,368,128]{2,1,0:T(8,128)(2,1)} %get-tuple-element.7), calls=%async_computation | async-start | bytes 1507328 | tf_op jit(solution)/shard_map/all_to_all | solution.py:433
  44.5 0.0 collective-permute-done.3.refs_5_.refs_6_
  44.5 0.0 copy-done.1
  44.5 0.0 copy-start.4
  44.5 0.0 collective-permute-done.1.refs_2_.refs_3_
  44.5 0.0 copy-done.2
  44.5 0.0 copy-start.5
  44.5 0.0 collective-permute-done.5.refs_7_.refs_8_
  44.5 0.0 copy-done.3
  44.5 0.6 copy-done.4
  45.2 0.1 copy-done.5
  45.3 0.0 copy-start.6
  45.3 0.7 copy-done.6
  46.0 0.0 collective-permute-done.2.refs_3_.refs_4_
  46.0 18.6 %rank.2.refs_0_ = bf16[800,512]{1,0:T(8,128)(2,1)} custom-call(s32[8,4,8]{2,1,0:T(4,128)} %counts_in_hbm.3, s32[8]{0:T(128)} %lengths_in_hbm.3, bf16[8,400,128]{2,1,0:T(8,128)(2,1)} %all-to-all-done.1.pieces, bf16[2,128,512]{2,1,0:T(8,128)(2,1)} %copy-done.1, bf16[2,128,512]{2,1,0:T(8,128)(2,1)} %copy-done.3, bf16[2,128,512]{2,1,0:T(8,128)(2,1)} %copy-done.5, ...), custom_call_target="tpu_custom_call" | custom-call | flops 20000000000 | bytes 20000000 | tf_op jit(solution)/shard_map/rank/pallas_call | solution.py:409
  64.6 0.0 all-to-all-done.pieces
  64.6 17.7 %rank.3 = bf16[1536,512]{1,0:T(8,128)(2,1)} custom-call(s32[8,4,8]{2,1,0:T(4,128)} %counts_in_hbm.3, s32[8]{0:T(128)} %lengths_in_hbm.3, bf16[8,368,128]{2,1,0:T(8,128)(2,1)} %all-to-all-done.pieces, bf16[800,512]{1,0:T(8,128)(2,1)} %rank.2.refs_0_, bf16[2,128,512]{2,1,0:T(8,128)(2,1)} %copy-done.1, bf16[2,128,512]{2,1,0:T(8,128)(2,1)} %copy-done.3, ...), custom_call_target="tpu_custom_call" | custom-call | flops 20000000000 | bytes 20000000 | tf_op jit(solution)/shard_map/rank/pallas_call | solution.py:409
Async XLA Ops:
  12.2 27.3 %all-to-all-start.1 = ((bf16[8,400,128]{2,1,0:T(8,128)(2,1)}), bf16[8,400,128]{2,1,0:T(8,128)(2,1)}, u32[]{:S(2)}, u32[]{:S(2)}) async-start(bf16[8,400,128]{2,1,0:T(8,128)(2,1)} %get-tuple-element.8), calls=%async_computation.1 | async-start | bytes 1638400 | tf_op jit(solution)/shard_map/all_to_all | solution.py:433
  19.7 2.5 %copy-start = (bf16[2,128,512]{2,1,0:T(8,128)(2,1)}, bf16[2,128,512]{2,1,0:T(8,128)(2,1)S(1)}, u32[]{:S(2)}) copy-start(bf16[2,128,512]{2,1,0:T(8,128)(2,1)S(1)} %get-tuple-element.9.refs_4_.refs_5_) | copy-start | bytes 786436
  19.7 24.8 %copy-start.1 = (bf16[2,128,512]{2,1,0:T(8,128)(2,1)}, bf16[2,128,512]{2,1,0:T(8,128)(2,1)S(1)}, u32[]{:S(2)}) copy-start(bf16[2,128,512]{2,1,0:T(8,128)(2,1)S(1)} %get-tuple-element.10.refs_0_.refs_1_) | copy-start | bytes 786436
  19.7 8.1 %collective-permute-start.4 = (bf16[2,128,512]{2,1,0:T(8,128)(2,1)S(1)}, bf16[2,128,512]{2,1,0:T(8,128)(2,1)S(1)}, u32[]{:S(2)}, u32[]{:S(2)}) collective-permute-start(bf16[2,128,512]{2,1,0:T(8,128)(2,1)S(1)} %get-tuple-element.9.refs_4_.refs_5_), channel_id=1, source_target_pairs={{0,2},{1,3},{2,0},{3,1},{4,6},{5,7},{6,4},{7,5},{8,10},{9,11},{10,... | collective-permute-start | bytes 786440 | tf_op jit(solution)/shard_map/ppermute | solution.py:140
  21.0 8.0 %collective-permute-start = (bf16[2,128,512]{2,1,0:T(8,128)(2,1)S(1)}, bf16[2,128,512]{2,1,0:T(8,128)(2,1)S(1)}, u32[]{:S(2)}, u32[]{:S(2)}) collective-permute-start(bf16[2,128,512]{2,1,0:T(8,128)(2,1)S(1)} %get-tuple-element.10.refs_0_.refs_1_), channel_id=1, source_target_pairs={{0,1},{1,0},{2,3},{3,2},{4,5},{5,4},{6,7},{7,6},{8,9},{9,8},{10,11... | collective-permute-start | bytes 786440 | tf_op jit(solution)/shard_map/ppermute | solution.py:140
  22.2 22.3 %collective-permute-start.3 = (bf16[2,128,512]{2,1,0:T(8,128)(2,1)S(1)}, bf16[2,128,512]{2,1,0:T(8,128)(2,1)S(1)}, u32[]{:S(2)}, u32[]{:S(2)}) collective-permute-start(bf16[2,128,512]{2,1,0:T(8,128)(2,1)S(1)} %get-tuple-element.9.refs_4_.refs_5_), channel_id=1, source_target_pairs={{0,1},{1,0},{2,3},{3,2},{4,5},{5,4},{6,7},{7,6},{8,9},{9,8},{10,11... | collective-permute-start | bytes 786440 | tf_op jit(solution)/shard_map/ppermute | solution.py:140
  22.5 22.0 %collective-permute-start.1 = (bf16[2,128,512]{2,1,0:T(8,128)(2,1)S(1)}, bf16[2,128,512]{2,1,0:T(8,128)(2,1)S(1)}, u32[]{:S(2)}, u32[]{:S(2)}) collective-permute-start(bf16[2,128,512]{2,1,0:T(8,128)(2,1)S(1)} %get-tuple-element.10.refs_0_.refs_1_), channel_id=1, source_target_pairs={{0,2},{1,3},{2,0},{3,1},{4,6},{5,7},{6,4},{7,5},{8,10},{9,11},{10,... | collective-permute-start | bytes 786440 | tf_op jit(solution)/shard_map/ppermute | solution.py:140
  27.8 16.7 %copy-start.2 = (bf16[2,128,512]{2,1,0:T(8,128)(2,1)}, bf16[2,128,512]{2,1,0:T(8,128)(2,1)S(1)}, u32[]{:S(2)}) copy-start(bf16[2,128,512]{2,1,0:T(8,128)(2,1)S(1)} %collective-permute-done.4.refs_6_.refs_7_) | copy-start | bytes 786436
  27.8 16.7 %collective-permute-start.5 = (bf16[2,128,512]{2,1,0:T(8,128)(2,1)S(1)}, bf16[2,128,512]{2,1,0:T(8,128)(2,1)S(1)}, u32[]{:S(2)}, u32[]{:S(2)}) collective-permute-start(bf16[2,128,512]{2,1,0:T(8,128)(2,1)S(1)} %collective-permute-done.4.refs_6_.refs_7_), channel_id=1, source_target_pairs={{0,1},{1,0},{2,3},{3,2},{4,5},{5,4},{6,7},{7,6},{8,9},{9,8},{10,11... | collective-permute-start | bytes 786440 | tf_op jit(solution)/shard_map/ppermute | solution.py:140
  29.0 15.5 %copy-start.3 = (bf16[2,128,512]{2,1,0:T(8,128)(2,1)}, bf16[2,128,512]{2,1,0:T(8,128)(2,1)S(1)}, u32[]{:S(2)}) copy-start(bf16[2,128,512]{2,1,0:T(8,128)(2,1)S(1)} %collective-permute-done.refs_1_.refs_2_) | copy-start | bytes 786436
  29.0 17.0 %collective-permute-start.2 = (bf16[2,128,512]{2,1,0:T(8,128)(2,1)S(1)}, bf16[2,128,512]{2,1,0:T(8,128)(2,1)}, u32[]{:S(2)}, u32[]{:S(2)}) collective-permute-start(bf16[2,128,512]{2,1,0:T(8,128)(2,1)S(1)} %collective-permute-done.refs_1_.refs_2_), channel_id=1, source_target_pairs={{0,2},{1,3},{2,0},{3,1},{4,6},{5,7},{6,4},{7,5},{8,10},{9,11},{10,... | collective-permute-start | bytes 786440 | tf_op jit(solution)/shard_map/ppermute | solution.py:140
  39.5 25.1 %all-to-all-start = ((bf16[8,368,128]{2,1,0:T(8,128)(2,1)}), bf16[8,368,128]{2,1,0:T(8,128)(2,1)}, u32[]{:S(2)}, u32[]{:S(2)}) async-start(bf16[8,368,128]{2,1,0:T(8,128)(2,1)} %get-tuple-element.7), calls=%async_computation | async-start | bytes 1507328 | tf_op jit(solution)/shard_map/all_to_all | solution.py:433
  44.5 0.7 copy-start.4
  44.5 0.8 copy-start.5
  45.3 0.7 copy-start.6
